TPU v7x, 256 devices: a whole 4x4x8 slice. The times are simulated.
256 devices in a mesh: grp: 2 (over core), row: 8 (over y_lo, x), tp: 16 (over z, y_hi).
Axes of the slice: x: 4, y: 4 (y_hi: 2, y_lo: 2; y = y_hi * 2 + y_lo), z: 8, core: 2. Of those that a mesh axis runs over, the one named last changes fastest.
Arguments:
- frame: bfloat16 [128, 16, 5120], P(('grp', 'row'), 'tp'), may hold values from -6 to 6
- cache: bfloat16 [128, 16, 512, 256], P(('grp', 'row'), 'tp'), may hold values from -6 to 6
- actions: int32 [128, 4], P(('grp', 'row')), may hold values from 0 to 17
- owners: int32 [128, 1], P(('grp', 'row')), may hold values from 0 to 7; in each aligned block of 8 rows (0 to 7, 8 to 15, ...) at most 2 rows name the same one
- attn_gain: float32 [5120], replicated, may hold values from 0.1 to 1.9
- w_query: bfloat16 [5120, 4096], P(None, 'tp'), may hold values from -1 to 1
- w_keyval: bfloat16 [5120, 2048], P(None, 'tp'), may hold values from -0.078125 to 0.078125
- w_out: bfloat16 [4096, 5120], P('tp'), may hold values from -0.09375 to 0.09375
- action_table: bfloat16 [18, 5120], replicated, may hold values from -6 to 6
- policy_in: bfloat16 [8, 5120, 2048], P('row', None, 'tp'), may hold values from -0.078125 to 0.078125
- policy_mid: bfloat16 [8, 2048, 2048], P('row', 'tp'), may hold values from -0.125 to 0.125
- policy_head: bfloat16 [8, 2048, 18], P('row'), may hold values from -0.25 to 0.25
- policy_value: bfloat16 [8, 2048], P('row'), may hold values from -0.125 to 0.125
Outputs:
- latents: bfloat16 [128, 16, 5120], P(('grp', 'row'), 'tp')
- log_probs: float32 [128, 4, 18], P(('grp', 'row'))
- values: float32 [128, 4], P(('grp', 'row'))
Inputs may be any that keep to these rules, and one draw needn't show every extreme that they name: `owners`: among the 8 rollouts of one device (aligned blocks of 8 rows), no policy is named by more than 2.
All inputs are finite; a program needn't handle non-finite values.
Results may differ from a plain program's by a relative error of at most 0.018.
Values may be sent and summed in bfloat16 or wider, within the bound.
A program may use at most 128 MiB of HBM per device.

v0:
```python
import jax
import jax.numpy as jnp
from jax import lax
from jax.sharding import PartitionSpec as P

KVH = 8
HD = 128
ACTIONS = 18
FRAME = 16
STEPS = 4
CAP = 2


EPS = 1e-05


def swapped(shard, axis, apart):
    return lax.ppermute(shard, axis, [(i, i ^ 1 << apart) for i in range(lax.axis_size(axis))])


def rms_rows(values):
    return values * lax.rsqrt(jnp.mean(values * values, axis=-1, keepdims=True) + EPS)


def shards(
    frame,
    cache,
    actions,
    owners,
    attn_gain,
    w_query,
    w_keyval,
    w_out,
    action_table,
    policy_in,
    policy_mid,
    policy_head,
    policy_value,
):
    n_tensor = lax.axis_size("tp")
    split = max(1, n_tensor // KVH)
    tensor_index = lax.axis_index("tp")
    rank = tensor_index % split
    rollouts = frame.shape[0]
    frame_local = frame.shape[1]
    width = frame.shape[2]
    heads_local = w_query.shape[1] // HD
    group_heads = heads_local * split
    kv_local = cache.shape[1]
    repeat = group_heads // kv_local
    own_rows = frame_local * rollouts
    keys_cache = cache[..., :HD]
    values_cache = cache[..., HD:]
    key_pos = jnp.arange(STEPS * FRAME, dtype=jnp.int32)
    key_step = key_pos // FRAME
    key_slot = key_pos % FRAME
    query_pos = jnp.arange(FRAME, dtype=jnp.int32)
    first = rank == 0
    owner = owners[:, 0]
    peers = lax.axis_size("row")
    owner_hit = (owner[:, None] == jnp.arange(peers, dtype=jnp.int32)[None, :]).astype(jnp.int32)
    place = jnp.cumsum(owner_hit, axis=0) - 1
    slot = jnp.sum(place * owner_hit, axis=1)
    slot_hit = (slot[None, :] == jnp.arange(CAP, dtype=jnp.int32)[:, None]).astype(jnp.int32)
    route = jnp.transpose(owner_hit)[:, None, :] * slot_hit[None, :, :]
    route_forward_backward = route.astype(jnp.bfloat16)
    route_forward_local = route.astype(jnp.float32)

    def decide(arrived):
        rows = arrived.reshape(-1, width)
        normed = rms_rows(rows.astype(jnp.float32)).astype(jnp.bfloat16)
        inner = jax.nn.silu(
            jnp.dot(normed, policy_in[0], preferred_element_type=jnp.float32)
        ).astype(jnp.bfloat16)
        partial_hidden = jnp.dot(inner, policy_mid[0], preferred_element_type=jnp.float32)
        hidden = jax.nn.silu(lax.psum(partial_hidden, "tp")).astype(jnp.bfloat16)
        logits = jnp.dot(hidden, policy_head[0], preferred_element_type=jnp.float32)
        value = jnp.dot(hidden, policy_value[0], preferred_element_type=jnp.float32)
        logp = logits - jax.nn.logsumexp(logits, axis=-1, keepdims=True)
        return (
            logp.reshape(arrived.shape[0], arrived.shape[1], -1),
            value.reshape(arrived.shape[0], arrived.shape[1]),
        )

    def act(gathered):
        latent_vector = gathered.reshape(FRAME, rollouts, width)[FRAME - 1]
        outgoing = jnp.einsum(
            "wmg,gh->wmh", route_forward_backward, latent_vector, preferred_element_type=jnp.float32
        ).astype(jnp.bfloat16)
        logp, value = decide(
            lax.all_to_all(outgoing, "row", split_axis=0, concat_axis=0, tiled=True)
        )
        returned_log_probability, returned_value_estimate = (
            lax.all_to_all(logp, "row", split_axis=0, concat_axis=0, tiled=True),
            lax.all_to_all(value, "row", split_axis=0, concat_axis=0, tiled=True),
        )
        local_log_probability = jnp.einsum(
            "ltw,lti->wi",
            route_forward_local,
            returned_log_probability,
            precision=lax.Precision.HIGHEST,
        )
        local_value_estimate = jnp.einsum(
            "qwv,qw->v",
            route_forward_local,
            returned_value_estimate,
            precision=lax.Precision.HIGHEST,
        )
        return (local_log_probability, local_value_estimate)

    start_rows = jnp.transpose(frame, (1, 0, 2)).reshape(own_rows, width)
    full = lax.all_gather(start_rows, "tp", axis=0, tiled=True)
    stash = jnp.zeros((rollouts, STEPS * FRAME, kv_local, 2 * HD), jnp.bfloat16)
    all_logp = []
    all_value = []
    pending = None
    for step in range(STEPS):
        world_stash = stash
        code = (actions[:, step][:, None] == jnp.arange(ACTIONS, dtype=jnp.int32)[None, :]).astype(
            jnp.bfloat16
        )
        embed = jnp.dot(code, action_table, preferred_element_type=jnp.float32)
        inputs = (full.reshape(FRAME, rollouts, width).astype(jnp.float32) + embed[None]).astype(
            jnp.bfloat16
        )
        flat = inputs.reshape(FRAME * rollouts, width)
        world_normed = (rms_rows(flat.astype(jnp.float32)) * attn_gain).astype(jnp.bfloat16)
        query = (
            jnp.dot(world_normed, w_query, preferred_element_type=jnp.float32) * HD ** (-0.5)
        ).astype(jnp.bfloat16)
        query = query.reshape(FRAME, rollouts, heads_local, HD)
        keyval = jnp.dot(world_normed, w_keyval, preferred_element_type=jnp.float32).astype(
            jnp.bfloat16
        )
        keyval = keyval.reshape(FRAME, rollouts, -1)
        bit = 0
        other_query, other_keyval = swapped((query, keyval), "tp", bit)
        lower = tensor_index >> bit & 1 == 0
        query = jnp.where(
            lower,
            jnp.concatenate([query, other_query], axis=2),
            jnp.concatenate([other_query, query], axis=2),
        )
        keyval = jnp.where(
            lower,
            jnp.concatenate([keyval, other_keyval], axis=2),
            jnp.concatenate([other_keyval, keyval], axis=2),
        )
        fresh = jnp.transpose(keyval.reshape(FRAME, rollouts, kv_local, 2 * HD), (1, 0, 2, 3))
        world_stash = world_stash.at[:, step * FRAME : (step + 1) * FRAME].set(fresh)
        grouped = query.reshape(FRAME, rollouts, kv_local, repeat, HD)
        score_cache = jnp.einsum(
            "frkgd,rkcd->rkgfc", grouped, keys_cache, preferred_element_type=jnp.float32
        )
        score_new = jnp.einsum(
            "frkgd,rjkd->rkgfj", grouped, world_stash[..., :HD], preferred_element_type=jnp.float32
        )
        allowed = (
            (key_step[None, :] < step)
            | (key_step[None, :] == step) & (key_slot[None, :] <= query_pos[:, None])
        ) & first
        score_new = jnp.where(allowed, score_new, -jnp.inf)
        top = jnp.maximum(jnp.max(score_cache, axis=-1), jnp.max(score_new, axis=-1))
        bit = 0
        other_top = swapped(top, "tp", bit)
        top = jnp.maximum(top, other_top)
        weight_cache = jnp.exp(score_cache - top[..., None])
        weight_new = jnp.exp(score_new - top[..., None])
        total = jnp.sum(weight_cache, axis=-1) + jnp.sum(weight_new, axis=-1)
        summed = jnp.einsum(
            "rkgfc,rkcd->rkgfd",
            weight_cache.astype(jnp.bfloat16),
            values_cache,
            preferred_element_type=jnp.float32,
        )
        summed = summed + jnp.einsum(
            "rkgfj,rjkd->rkgfd",
            weight_new.astype(jnp.bfloat16),
            world_stash[..., HD:],
            preferred_element_type=jnp.float32,
        )
        bit = 0
        other_summed, other_total = swapped((summed, total), "tp", bit)
        summed = summed + other_summed
        total = total + other_total
        attended = summed / total[..., None]
        attended = jnp.transpose(attended, (3, 0, 1, 2, 4)).reshape(
            FRAME * rollouts, group_heads * HD
        )
        attended = lax.dynamic_slice_in_dim(
            attended, rank * heads_local * HD, heads_local * HD, 1
        ).astype(jnp.bfloat16)
        terms = jnp.dot(attended, w_out, preferred_element_type=jnp.float32)
        reduced = lax.psum_scatter(terms, "tp", scatter_dimension=1, tiled=True)
        columns = reduced.shape[1]
        residual = lax.dynamic_slice_in_dim(flat, tensor_index * columns, columns, 1)
        updated = (residual.astype(jnp.float32) + reduced).astype(jnp.bfloat16)
        world_gathered = lax.all_gather(updated, "tp", axis=1, tiled=True)
        full = world_gathered
        stash = world_stash
        if pending is not None:
            logp, value = act(pending)
            all_logp.append(logp)
            all_value.append(value)
        pending = full
    logp, value = act(pending)
    all_logp.append(logp)
    all_value.append(value)
    own_part = lax.dynamic_slice_in_dim(full, tensor_index * own_rows, own_rows, 0)
    latents = jnp.transpose(own_part.reshape(frame_local, rollouts, width), (1, 0, 2))
    return (latents, jnp.stack(all_logp, axis=1), jnp.stack(all_value, axis=1))


def solution(mesh):
    placed = (
        P(("grp", "row"), "tp", None),
        P(("grp", "row"), "tp", None, None),
        P(("grp", "row"), None),
        P(("grp", "row"), None),
        P(),
        P(None, "tp"),
        P(None, "tp"),
        P("tp", None),
        P(),
        P("row", None, "tp"),
        P("row", "tp", None),
        P("row", None, None),
        P("row", None),
    )
    return jax.shard_map(
        shards,
        mesh=mesh,
        in_specs=placed,
        out_specs=(
            P(("grp", "row"), "tp", None),
            P(("grp", "row"), None, None),
            P(("grp", "row"), None),
        ),
        check_vma=False,
    )
```

profile of v0, /device:TPU:8, one launch (start us, length us, event | category | flops | bytes accessed | tf_op | source)
XLA Modules:
  0.0 1655.3 jit_solution(10918464242421161476)
XLA Ops:
  11.7 3.2 copy.166
  15.0 78.1 %all-gather.15.cloned.1.call-done = bf16[128,1,5120]{2,0,1:T(8,128)(2,1)} async-done(((bf16[8,1,5120]{2,0,1:T(8,128)(2,1)}), bf16[128,1,5120]{2,0,1:T(8,128)(2,1)}) %all-gather.15.cloned.1.call-update) | async-done | bytes 1310736 | tf_op jit(solution)/shard_map/all_gather | solution.py:112
  105.4 3.2 collective-permute-done
  111.7 3.2 collective-permute-done.2
  119.8 4.5 collective-permute-done.4
  127.4 210.1 %reduce-scatter.5.cloned.1.call-done = f32[128,320]{0,1:T(8,128)} async-done(((f32[128,5120]{0,1:T(8,128)}), f32[128,320]{0,1:T(8,128)}) %reduce-scatter.5.cloned.1.call-update) | async-done | bytes 163856 | tf_op jit(solution)/shard_map/reduce_scatter | solution.py:194
  341.2 3.2 copy.176
  344.4 74.8 %all-gather.7.cloned.1.call-done = bf16[128,5120]{0,1:T(8,128)(2,1)} async-done(((bf16[128,320]{0,1:T(8,128)(2,1)}), bf16[128,5120]{0,1:T(8,128)(2,1)}) %all-gather.7.cloned.1.call-update) | async-done | bytes 1310736 | tf_op jit(solution)/shard_map/all_gather | solution.py:198
  419.2 2.9 fusion.3
  429.4 3.2 collective-permute-done.5
  435.8 3.2 collective-permute-done.7
  443.9 4.5 collective-permute-done.9
  451.4 210.1 %reduce-scatter.7.cloned.1.call-done = f32[128,320]{0,1:T(8,128)} async-done(((f32[128,5120]{0,1:T(8,128)}), f32[128,320]{0,1:T(8,128)}) %reduce-scatter.7.cloned.1.call-update) | async-done | bytes 163856 | tf_op jit(solution)/shard_map/reduce_scatter | solution.py:194
  665.2 3.2 copy.184
  668.4 74.7 %all-gather.9.cloned.1.call-done = bf16[128,5120]{0,1:T(8,128)(2,1)} async-done(((bf16[128,320]{0,1:T(8,128)(2,1)}), bf16[128,5120]{0,1:T(8,128)(2,1)}) %all-gather.9.cloned.1.call-update) | async-done | bytes 1310736 | tf_op jit(solution)/shard_map/all_gather | solution.py:198
  743.1 2.9 fusion.6
  752.9 3.2 collective-permute-done.10
  759.4 3.2 collective-permute-done.12
  767.6 4.5 collective-permute-done.14
  775.1 210.1 %reduce-scatter.9.cloned.1.call-done = f32[128,320]{0,1:T(8,128)} async-done(((f32[128,5120]{0,1:T(8,128)}), f32[128,320]{0,1:T(8,128)}) %reduce-scatter.9.cloned.1.call-update) | async-done | bytes 163856 | tf_op jit(solution)/shard_map/reduce_scatter | solution.py:194
  988.9 3.2 copy.192
  992.1 74.7 %all-gather.11.cloned.1.call-done = bf16[128,5120]{0,1:T(8,128)(2,1)} async-done(((bf16[128,320]{0,1:T(8,128)(2,1)}), bf16[128,5120]{0,1:T(8,128)(2,1)}) %all-gather.11.cloned.1.call-update) | async-done | bytes 1310736 | tf_op jit(solution)/shard_map/all_gather | solution.py:198
  1076.6 3.2 collective-permute-done.15
  1082.9 3.2 collective-permute-done.17
  1091.3 4.3 collective-permute-done.19
  1102.4 5.7 all-to-all-start
  1108.1 5.3 all-to-all-done
  1118.3 4.8 all-to-all-start.2
  1128.7 180.0 %reduce-scatter.11.cloned.1.call-done = f32[128,320]{0,1:T(8,128)} async-done(((f32[128,5120]{0,1:T(8,128)}), f32[128,320]{0,1:T(8,128)}) %reduce-scatter.11.cloned.1.call-update) | async-done | bytes 163856 | tf_op jit(solution)/shard_map/reduce_scatter | solution.py:194
  1315.1 5.7 all-to-all-start.4
  1328.2 62.1 %all-gather.13.cloned.1.call-done = bf16[128,5120]{0,1:T(8,128)(2,1)} async-done(((bf16[128,320]{0,1:T(8,128)(2,1)}), bf16[128,5120]{0,1:T(8,128)(2,1)}) %all-gather.13.cloned.1.call-update) | async-done | bytes 1310736 | tf_op jit(solution)/shard_map/all_gather | solution.py:198
  1393.2 5.7 all-to-all-start.6
  1412.4 150.0 %all-reduce.4.cloned.1.call-done = (f32[16,2048]{1,0:T(8,128)}, f32[16,2048]{1,0:T(8,128)}, f32[16,2048]{1,0:T(8,128)}, f32[16,2048]{1,0:T(8,128)}) async-done(((f32[16,2048]{1,0:T(8,128)}, f32[16,2048]{1,0:T(8,128)}, f32[16,2048]{1,0:T(8,128)}, f32[16,2048]{1,0:T(8,128)}), (f32[16,2048]{1,0:T(8,128)}, f32[16,2048]{1,0:T(8,128)}, f32[16,2048]{1,0:T(8,128)}, ...) | async-done | bytes 524304 | tf_op jit(solution)/shard_map/psum | solution.py:76
  1568.4 5.7 all-to-all-start.11
  1580.5 5.7 all-to-all-start.10
  1586.5 4.3 all-to-all-done.10
  1590.8 4.7 all-to-all-start.9
  1595.7 4.4 all-to-all-done.9
  1600.2 4.7 all-to-all-start.8
  1605.1 4.4 all-to-all-done.8
  1609.5 4.7 all-to-all-start.1
  1615.1 3.9 all-to-all-done.1
  1619.0 4.7 all-to-all-start.3
  1623.9 4.5 all-to-all-done.3
  1628.4 4.7 all-to-all-start.5
  1633.4 4.5 all-to-all-done.5
  1637.8 4.7 all-to-all-start.7
  1642.8 4.5 all-to-all-done.7
  (287 shorter events, 155.8 us)
Async XLA Ops:
  7.2 117.5 %copy-start = (bf16[256,5120]{1,0:T(8,128)(2,1)S(1)}, bf16[256,5120]{1,0:T(8,128)(2,1)}, u32[]{:S(2)}) copy-start(bf16[256,5120]{1,0:T(8,128)(2,1)} %param.28) | copy-start | bytes 7864324
  7.2 86.0 %all-gather.15.cloned.1.call-start = ((), (), s32[]{:S(2)}) async-start(), calls=%async_computation.24 | async-start | bytes 1392640 | tf_op jit(solution)/shard_map/all_gather | solution.py:112
  7.9 329.6 %reduce-scatter.5.cloned.1.call-start = ((), (), s32[]{:S(2)}) async-start(), calls=%async_computation.16 | async-start | bytes 2785280 | tf_op jit(solution)/shard_map/reduce_scatter | solution.py:194
  99.9 5.5 collective-permute-start.1
  102.8 5.9 collective-permute-start
  109.5 5.4 collective-permute-start.2
  116.2 8.1 collective-permute-start.3
  118.4 5.9 collective-permute-start.4
  127.3 211.9 %copy-start.6 = (bf16[18,5120]{1,0:T(8,128)(2,1)S(1)}, bf16[18,5120]{1,0:T(8,128)(2,1)}, u32[]{:S(2)}) copy-start(bf16[18,5120]{1,0:T(8,128)(2,1)} %param.29) | copy-start | bytes 552964
  127.3 291.8 %all-gather.7.cloned.1.call-start = ((), (), s32[]{:S(2)}) async-start(), calls=%async_computation.17 | async-start | bytes 1392640 | tf_op jit(solution)/shard_map/all_gather | solution.py:198
  339.1 322.4 %reduce-scatter.7.cloned.1.call-start = ((), (), s32[]{:S(2)}) async-start(), calls=%async_computation.18 | async-start | bytes 2785280 | tf_op jit(solution)/shard_map/reduce_scatter | solution.py:194
  423.4 9.2 copy-start.2
  423.5 6.0 collective-permute-start.6
  426.8 5.9 collective-permute-start.5
  433.6 5.4 collective-permute-start.7
  440.3 8.1 collective-permute-start.8
  442.5 5.9 collective-permute-start.9
  451.4 291.7 %all-gather.9.cloned.1.call-start = ((), (), s32[]{:S(2)}) async-start(), calls=%async_computation.19 | async-start | bytes 1392640 | tf_op jit(solution)/shard_map/all_gather | solution.py:198
  663.2 322.0 %reduce-scatter.9.cloned.1.call-start = ((), (), s32[]{:S(2)}) async-start(), calls=%async_computation.20 | async-start | bytes 2785280 | tf_op jit(solution)/shard_map/reduce_scatter | solution.py:194
  747.4 5.5 collective-permute-start.11
  750.3 5.9 collective-permute-start.10
  757.0 5.6 collective-permute-start.12
  763.9 8.1 collective-permute-start.13
  766.2 5.9 collective-permute-start.14
  775.0 291.8 %all-gather.11.cloned.1.call-start = ((), (), s32[]{:S(2)}) async-start(), calls=%async_computation.21 | async-start | bytes 1392640 | tf_op jit(solution)/shard_map/all_gather | solution.py:198
  986.8 321.9 %reduce-scatter.11.cloned.1.call-start = ((), (), s32[]{:S(2)}) async-start(), calls=%async_computation.22 | async-start | bytes 2785280 | tf_op jit(solution)/shard_map/reduce_scatter | solution.py:194
  1071.1 5.5 collective-permute-start.16
  1074.0 5.9 collective-permute-start.15
  1080.7 5.4 collective-permute-start.17
  1087.5 8.1 collective-permute-start.18
  1089.7 5.9 collective-permute-start.19
  1101.5 21.6 %copy-start.5 = (bf16[1,128,2048]{2,1,0:T(8,128)(2,1)S(1)}, bf16[1,128,2048]{2,1,0:T(8,128)(2,1)}, u32[]{:S(2)}) copy-start(bf16[1,128,2048]{2,1,0:T(8,128)(2,1)} %param.31) | copy-start | bytes 1572868
  1102.4 11.0 all-to-all-start
  1118.3 10.1 all-to-all-start.2
  1123.1 267.3 %all-gather.13.cloned.1.call-start = ((), (), s32[]{:S(2)}) async-start(), calls=%async_computation.23 | async-start | bytes 1392640 | tf_op jit(solution)/shard_map/all_gather | solution.py:198
  1315.1 11.0 all-to-all-start.4
  1393.2 11.0 all-to-all-start.6
  1398.9 163.5 %all-reduce.4.cloned.1.call-start = ((), (), s32[]{:S(2)}) async-start(), calls=%async_computation.25 | async-start | bytes 1048576 | tf_op jit(solution)/shard_map/psum | solution.py:76
  1407.2 157.2 %copy-start.7 = (bf16[1,2048,18]{1,2,0:T(8,128)(2,1)S(1)}, bf16[1,2048,18]{1,2,0:T(8,128)(2,1)}, u32[]{:S(2)}) copy-start(bf16[1,2048,18]{1,2,0:T(8,128)(2,1)} %param.32) | copy-start | bytes 221188
  1410.1 157.4 %copy-start.22 = (bf16[1,2048]{1,0:T(2,128)(2,1)S(1)}, bf16[1,2048]{1,0:T(2,128)(2,1)}, u32[]{:S(2)}) copy-start(bf16[1,2048]{1,0:T(2,128)(2,1)} %param.33) | copy-start | bytes 12292
  1568.4 12.1 all-to-all-start.11
  1580.5 10.2 all-to-all-start.10
  1590.8 9.4 all-to-all-start.9
  1600.2 9.3 all-to-all-start.8
  1609.5 9.5 all-to-all-start.1
  1619.0 9.4 all-to-all-start.3
  1628.4 9.4 all-to-all-start.5
  1637.8 9.5 all-to-all-start.7
  (17 other events, 71.0 us)
Sparse Core Ops, SparseCore 0:
  10.6 82.5 all-gather.14
  127.4 209.9 reduce-scatter.4
  340.7 78.4 all-gather.6
  451.5 209.9 reduce-scatter.6
  664.5 78.5 all-gather.8
  775.2 209.9 reduce-scatter.8
  988.4 78.3 all-gather.10
  1098.7 209.9 reduce-scatter.10
  1311.9 78.4 all-gather.12
  1407.3 154.9 all-reduce.3
where the time goes:
time: 1670 us; the launch traced here: 1660 us
  waiting for transfers between devices  1420 us (85%)
  starting transfers between devices  101 us (6%)
  matrix products  50.7 us (3%)
  local copies, waits for them, and re-layouts  39.9 us (2%)
  other arithmetic  33.6 us (2%)
    reduce_scatter x4, waiting for transfers between devices, shards(): reduced = lax.psum_scatter(terms, 'tp', scatter_dimension=1, tiled=True)  810 us
    all_gather x4, waiting for transfers between devices, shards(): world_gathered = lax.all_gather(updated, 'tp', axis=1, tiled=True)  286 us
    psum x1, waiting for transfers between devices, decide(): hidden = jax.nn.silu(lax.psum(partial_hidden, 'tp')).astype(jnp.bfloat16)  150 us
    all_gather x1, waiting for transfers between devices, shards(): full = lax.all_gather(start_rows, 'tp', axis=0, tiled=True)  78.1 us
    ppermute x20, waiting for transfers between devices, swapped(): lax.ppermute(shard, axis, [(i, i ^ 1 << apart) for i in range(lax.axis_si...  45.3 us
    ppermute x20, starting transfers between devices, swapped(): lax.ppermute(shard, axis, [(i, i ^ 1 << apart) for i in range(lax.axis_si...  38.9 us
  transfers between devices with their start and end apart: 42, of which 37 were waited for; matrix products, arithmetic and copies ran while one was open for 4% of the time, Pallas kernels for 0%

commit v1 on v0

v1 whole, which is shorter than its diff:
```python
import functools

import jax
import jax.numpy as jnp
from jax import lax
from jax.experimental import pallas as pl
from jax.experimental.pallas import tpu as pltpu
from jax.sharding import PartitionSpec as P

HD = 128
STEPS = 4
CAP = 2
EPS = 1e-05
MESH = pl.DeviceIdType.MESH
F32 = jnp.float32
BF16 = jnp.bfloat16
VMEM_LIMIT = 56 << 20


def rms_rows(values):
    return values * lax.rsqrt(jnp.mean(values * values, axis=-1, keepdims=True) + EPS)


def folded(rows):
    half = rows.shape[1] // 2
    return jnp.concatenate([rows[:, :half], rows[:, half:]], axis=0)


def halves(product, half, width):
    return product.reshape(-1, 2, 8, width)[:, half].reshape(-1, width)


def fold_dot(chunks, weight):
    half = weight.shape[0] // 2
    columns = weight.shape[1]
    left = jnp.dot(chunks, weight[:half], preferred_element_type=F32)
    right = jnp.dot(chunks, weight[half:], preferred_element_type=F32)
    return halves(left, 0, columns) + halves(right, 1, columns)


def world_kernel(
    n_z,
    frame_ref,
    actions_ref,
    gain_ref,
    table_ref,
    cache_ref,
    wq_ref,
    wkv_ref,
    wo_ref,
    latents_ref,
    rows_ref,
    state,
    gath,
    qkv,
    qkv_in,
    keys,
    vals,
    scores,
    weights,
    own_o,
    out_o,
    in_o,
    terms,
    pair_in,
    zsum,
    zsum_in,
    ag_send,
    ag_recv,
    fw_send,
    fw_recv,
    z_send,
    z_recv,
    q_send,
    q_recv,
    o_send,
    o_recv,
    p_send,
    p_recv,
    s_send,
    s_recv,
):
    tensor = lax.axis_index("tp")
    z = tensor // 2
    yh = lax.rem(tensor, 2)
    partner = tensor + 1 - 2 * yh
    rollouts, width = state.shape
    tokens = 2 * n_z
    n_rows = tokens * rollouts
    cached = cache_ref.shape[2]
    last = tokens - 1
    order = [k for d in range(1, n_z // 2 + 1) for k in dict.fromkeys((d, n_z - d))]

    def plane(k):
        return lax.rem(z + k, n_z)

    def to_plane(k):
        return {"tp": plane(k) * 2 + yh}

    barrier = pltpu.get_barrier_semaphore()
    for k in order:
        pl.semaphore_signal(barrier, inc=1, device_id=to_plane(k), device_id_type=MESH)
    pl.semaphore_signal(barrier, inc=1, device_id={"tp": partner}, device_id_type=MESH)

    def copy(src, dst, send, recv, target):
        return pltpu.make_async_remote_copy(
            src_ref=src, dst_ref=dst, send_sem=send, recv_sem=recv, device_id=target, device_id_type=MESH
        )

    state[...] = frame_ref[...].astype(F32)
    keys[...] = jnp.zeros_like(keys)
    vals[...] = jnp.zeros_like(vals)
    iota_r = lax.broadcasted_iota(jnp.int32, (n_rows, n_rows), 0)
    iota_c = lax.broadcasted_iota(jnp.int32, (n_rows, n_rows), 1)
    by_rollout = (lax.rem(iota_r, tokens) * rollouts + iota_r // tokens == iota_c).astype(F32).astype(BF16)
    by_token = (lax.rem(iota_c, tokens) * rollouts + iota_c // tokens == iota_r).astype(F32).astype(BF16)
    pl.semaphore_wait(barrier, len(order) + 1)

    def spread_rows(s):
        source = rows_ref.at[s]

        def across(k):
            return copy(source, source, z_send.at[s, k], z_recv.at[s, 0], to_plane(k))

        pair = copy(source, source, z_send.at[s, 0], z_recv.at[s, 1], {"tp": partner})

        def start():
            @pl.when(tensor == last)
            def _():
                for k in order:
                    across(k).start()
                pair.start()

        def finish():
            @pl.when((yh == 1) & (tensor != last))
            def _():
                across(1).wait_recv()
                pair.start()

            @pl.when(yh == 0)
            def _():
                pair.wait_recv()

            @pl.when(yh == 1)
            def _():
                pair.wait_send()

            @pl.when(tensor == last)
            def _():
                for k in order:
                    across(k).wait_send()

        return start, finish

    def step(s, carry):
        picked = jnp.sum(
            jnp.where(lax.broadcasted_iota(jnp.int32, actions_ref.shape, 1) == s, actions_ref[...], 0),
            axis=1,
            keepdims=True,
        )
        code = (lax.broadcasted_iota(jnp.int32, (rollouts, table_ref.shape[0]), 1) == picked).astype(F32).astype(BF16)
        embed = jnp.dot(code, table_ref[...], preferred_element_type=F32)
        inputs = (state[...] + embed).astype(BF16).astype(F32)
        state[...] = inputs
        normed = rms_rows(inputs) * gain_ref[...]
        gath[s, tensor] = folded(normed).astype(BF16)

        mine = gath.at[s, tensor]
        for k in order:
            copy(mine, mine, ag_send.at[s, k], ag_recv.at[s, k], to_plane(k)).start()
        forward = {}
        for k in [0] + order:
            slot = gath.at[s, plane(k) * 2 + yh]
            if k:
                copy(slot, slot, ag_send.at[s, n_z - k], ag_recv.at[s, n_z - k], to_plane(k)).wait_recv()
            forward[k] = copy(slot, slot, fw_send.at[s, k], fw_recv.at[s, k], {"tp": partner})
            forward[k].start()
        for k in [0] + order:
            slot = gath.at[s, plane(k) * 2 + 1 - yh]
            copy(slot, slot, fw_send.at[s, k], fw_recv.at[s, k], {"tp": partner}).wait_recv()

        chunks = gath[s].reshape(tokens * 16, width // 2)
        query = (fold_dot(chunks, wq_ref) * HD ** (-0.5)).astype(BF16)
        keyval = fold_dot(chunks, wkv_ref).astype(BF16)
        n_query = query.shape[1]
        qkv[s, :, :n_query] = jnp.dot(by_rollout, query, preferred_element_type=F32).astype(BF16)
        qkv[s, :, n_query:] = jnp.dot(by_rollout, keyval, preferred_element_type=F32).astype(BF16)
        swap = copy(qkv.at[s], qkv_in.at[s], q_send.at[s], q_recv.at[s], {"tp": partner})
        swap.start()
        for k in order:
            copy(mine, mine, ag_send.at[s, k], ag_recv.at[s, k], to_plane(k)).wait_send()
        for k in [0] + order:
            forward[k].wait_send()
        swap.wait()

        own_kv = qkv[s, :, n_query:].astype(F32)
        other_kv = qkv_in[s, :, n_query:].astype(F32)
        new_key = jnp.where(yh == 0, own_kv, other_kv).astype(BF16)
        new_val = jnp.where(yh == 0, other_kv, own_kv).astype(BF16)
        place = pl.ds(pl.multiple_of(s * tokens, tokens), tokens)
        heads = n_query // HD
        per = 2 * heads * tokens
        nt = (((1,), (1,)), ((), ()))
        for r in range(rollouts):
            rows = slice(r * tokens, (r + 1) * tokens)
            keys[r, place, :] = new_key[rows]
            vals[r, place, :] = new_val[rows]
            parts = [qkv[s, rows, h * HD : (h + 1) * HD] for h in range(heads)]
            parts += [qkv_in[s, rows, h * HD : (h + 1) * HD] for h in range(heads)]
            grouped = jnp.concatenate(parts, axis=0)
            band = slice(r * per, (r + 1) * per)
            scores[band, :cached] = lax.dot_general(
                grouped, cache_ref[r, 0, :, :HD], nt, preferred_element_type=F32
            )
            scores[band, cached:] = lax.dot_general(grouped, keys[r], nt, preferred_element_type=F32)
        fresh = scores[:, cached:]
        key_pos = lax.broadcasted_iota(jnp.int32, fresh.shape, 1)
        query_pos = lax.rem(lax.broadcasted_iota(jnp.int32, fresh.shape, 0), tokens)
        allowed = (key_pos <= s * tokens + query_pos) & (yh == 0)
        fresh = jnp.where(allowed, fresh, -jnp.inf)
        old = scores[:, :cached]
        top = jnp.maximum(jnp.max(old, axis=1, keepdims=True), jnp.max(fresh, axis=1, keepdims=True))
        old = jnp.exp(old - top)
        fresh = jnp.exp(fresh - top)
        total = jnp.sum(old, axis=1, keepdims=True) + jnp.sum(fresh, axis=1, keepdims=True)
        weights[:, :cached] = old.astype(BF16)
        weights[:, cached:] = fresh.astype(BF16)
        inverse = 1.0 / total
        lane = lax.broadcasted_iota(jnp.int32, (tokens, HD), 1)
        for r in range(rollouts):
            rows = slice(r * tokens, (r + 1) * tokens)
            band = slice(r * per, (r + 1) * per)
            summed = jnp.dot(weights[band, :cached], cache_ref[r, 0, :, HD:], preferred_element_type=F32)
            summed = summed + jnp.dot(weights[band, cached:], vals[r], preferred_element_type=F32)
            summed = summed * inverse[band]
            stats = jnp.zeros((tokens, HD), F32)
            for h in range(heads):
                own_o[rows, h * HD : (h + 1) * HD] = summed[h * tokens : (h + 1) * tokens]
                far = slice((heads + h) * tokens, (heads + h + 1) * tokens)
                out_o[s, rows, h * HD : (h + 1) * HD] = summed[far].astype(BF16)
                left = top[band][far]
                for piece in range(3):
                    term = left.astype(BF16).astype(F32)
                    left = left - term
                    stats = jnp.where(lane == 8 * h + piece, term, stats)
                left = total[band][far]
                for piece in range(3):
                    term = left.astype(BF16).astype(F32)
                    left = left - term
                    stats = jnp.where(lane == 8 * h + 3 + piece, term, stats)
            out_o[s, rows, n_query:] = stats.astype(BF16)
        swap = copy(out_o.at[s], in_o.at[s], o_send.at[s], o_recv.at[s], {"tp": partner})
        swap.start()
        swap.wait()

        stats = in_o[s, :, n_query:].astype(F32)
        top4 = top.reshape(rollouts, 2 * heads, tokens, 1)
        total4 = total.reshape(rollouts, 2 * heads, tokens, 1)
        joined = []
        for h in range(heads):
            pick = [stats[:, 8 * h + i : 8 * h + i + 1] for i in range(6)]
            far_top = pick[0] + pick[1] + pick[2]
            far_total = pick[3] + pick[4] + pick[5]
            near_top = top4[:, h].reshape(n_rows, 1)
            near_total = total4[:, h].reshape(n_rows, 1)
            peak = jnp.maximum(near_top, far_top)
            near = near_total * jnp.exp(near_top - peak)
            far = far_total * jnp.exp(far_top - peak)
            both = 1.0 / (near + far)
            cols = slice(h * HD, (h + 1) * HD)
            joined.append(own_o[:, cols] * (near * both) + in_o[s, :, cols].astype(F32) * (far * both))
        attended = jnp.concatenate(joined, axis=1).astype(BF16)
        attended = jnp.dot(by_token, attended, preferred_element_type=F32).astype(BF16)

        tile = 512 if (width // 2) % 512 == 0 else HD
        for j in range(width // 2 // tile):
            at = slice(j * tile, (j + 1) * tile)
            also = slice(width // 2 + j * tile, width // 2 + (j + 1) * tile)
            left = jnp.dot(attended, wo_ref[:, at], preferred_element_type=F32).reshape(tokens, rollouts, tile)
            right = jnp.dot(attended, wo_ref[:, also], preferred_element_type=F32).reshape(tokens, rollouts, tile)
            terms[:, :, at] = jnp.concatenate([left, right], axis=1).astype(BF16)

        def to_pair(k):
            return copy(
                terms.at[plane(k) * 2 + 1 - yh], pair_in.at[s, k], p_send.at[s, k], p_recv.at[s, k], {"tp": partner}
            )

        def across(k):
            return copy(zsum.at[k], zsum_in.at[s, k], s_send.at[s, k], s_recv.at[s, k], to_plane(k))

        outward = order[::-1]
        for k in outward + [0]:
            to_pair(k).start()
        for k in outward:
            to_pair(k).wait_recv()
            zsum[k] = (terms[plane(k) * 2 + yh].astype(F32) + pair_in[s, k].astype(F32)).astype(BF16)
            across(k).start()
        to_pair(0).wait_recv()
        reduced = terms[tensor].astype(F32) + pair_in[s, 0].astype(F32)
        for k in order:
            across(n_z - k).wait_recv()
            reduced = reduced + zsum_in[s, n_z - k].astype(F32)
        reduced = jnp.concatenate([reduced[:rollouts], reduced[rollouts:]], axis=1)
        updated = (state[...] + reduced).astype(BF16).astype(F32)
        state[...] = updated

        @pl.when(tensor == last)
        def _():
            rows_ref[s] = folded(rms_rows(updated)).astype(BF16)

        start, finish = spread_rows(s)
        start()
        for k in outward:
            to_pair(k).wait_send()
            across(k).wait_send()
        to_pair(0).wait_send()
        finish()
        return carry

    lax.fori_loop(0, STEPS, step, 0)
    latents_ref[...] = state[...].astype(BF16)


def policy_kernel(
    peers,
    n_tensor,
    rows_ref,
    owners_ref,
    pin_ref,
    pmid_ref,
    head_ref,
    critic_ref,
    logp_ref,
    value_ref,
    outgoing,
    arrived,
    partial,
    partial_in,
    hidden,
    answers,
    returned,
    a_send,
    a_recv,
    h_send,
    h_recv,
    g_send,
    g_recv,
    b_send,
    b_recv,
):
    tensor = lax.axis_index("tp")
    row = lax.axis_index("row")
    rollouts = owners_ref.shape[0]
    actions = head_ref.shape[1]
    per = STEPS * CAP

    def to_row(k):
        return {"row": lax.rem(row + k, peers)}

    def to_tensor(k):
        return {"tp": lax.rem(tensor + k, n_tensor)}

    barrier = pltpu.get_barrier_semaphore()
    for k in range(1, peers):
        pl.semaphore_signal(barrier, inc=1, device_id=to_row(k), device_id_type=MESH)
    for k in range(1, n_tensor):
        pl.semaphore_signal(barrier, inc=1, device_id=to_tensor(k), device_id_type=MESH)

    def copy(src, dst, send, recv, target):
        return pltpu.make_async_remote_copy(
            src_ref=src, dst_ref=dst, send_sem=send, recv_sem=recv, device_id=target, device_id_type=MESH
        )

    owner_col = owners_ref[...]
    hit = (lax.broadcasted_iota(jnp.int32, (rollouts, 128), 1) == owner_col).astype(F32)
    lower = (
        lax.broadcasted_iota(jnp.int32, (rollouts, rollouts), 0)
        > lax.broadcasted_iota(jnp.int32, (rollouts, rollouts), 1)
    ).astype(F32)
    before = jnp.zeros((rollouts, 128), F32)
    for r in range(rollouts):
        before = before + lower[:, r : r + 1] * hit[r : r + 1, :]
    slot = jnp.sum(before * hit, axis=1, keepdims=True)
    places = peers * per
    col = lax.broadcasted_iota(jnp.int32, (rollouts, places), 1)
    owner_hit = (col // per == owner_col) & (lax.rem(col, CAP).astype(F32) == slot)
    step_of = lax.rem(col, per) // CAP
    hot = jnp.concatenate([(owner_hit & (step_of == s)).astype(F32) for s in range(STEPS)], axis=0)
    hot16 = hot.astype(BF16)
    tn = (((0,), (0,)), ((), ()))
    sources = rows_ref[...].astype(F32).reshape(STEPS, 2, rollouts, -1)
    half = sources.shape[-1]
    left = lax.dot_general(
        hot16, sources[:, 0].reshape(STEPS * rollouts, half).astype(BF16), tn, preferred_element_type=F32
    )
    right = lax.dot_general(
        hot16, sources[:, 1].reshape(STEPS * rollouts, half).astype(BF16), tn, preferred_element_type=F32
    )
    outgoing[...] = jnp.concatenate(
        [left.reshape(peers, per, half), right.reshape(peers, per, half)], axis=1
    ).astype(BF16)
    arrived[row] = outgoing[row]
    pl.semaphore_wait(barrier, peers + n_tensor - 2)

    def route(k):
        return copy(outgoing.at[lax.rem(row + k, peers)], arrived.at[row], a_send.at[k], a_recv.at[k], to_row(k))

    for k in range(1, peers):
        route(k).start()
    for k in range(1, peers):
        origin = lax.rem(row + peers - k, peers)
        copy(arrived.at[origin], arrived.at[origin], a_send.at[k], a_recv.at[k], to_row(k)).wait_recv()
    chunks = arrived[...].reshape(peers * 16, half)
    inner = jax.nn.silu(fold_dot(chunks, pin_ref.at[0])).astype(BF16)
    units = pmid_ref.shape[2] // n_tensor
    for j in range(n_tensor):
        partial[j] = jnp.dot(
            inner, pmid_ref[0, :, j * units : (j + 1) * units], preferred_element_type=F32
        ).astype(BF16)

    def to_units(k):
        return copy(
            partial.at[lax.rem(tensor + k, n_tensor)], partial_in.at[k], h_send.at[k], h_recv.at[k], to_tensor(k)
        )

    for k in range(1, n_tensor):
        to_units(k).start()
    summed = partial[tensor].astype(F32)
    for k in range(1, n_tensor):
        to_units(k).wait_recv()
        summed = summed + partial_in[k].astype(F32)
    hidden[tensor] = jax.nn.silu(summed).astype(BF16)

    def share(k):
        return copy(hidden.at[tensor], hidden.at[tensor], g_send.at[k], g_recv.at[k], to_tensor(k))

    for k in range(1, n_tensor):
        share(k).start()
    for k in range(1, n_tensor):
        origin = lax.rem(tensor + n_tensor - k, n_tensor)
        copy(hidden.at[origin], hidden.at[origin], g_send.at[k], g_recv.at[k], to_tensor(k)).wait_recv()
    logits = jnp.zeros((places, actions), F32)
    value = jnp.zeros((places, 1), F32)
    for j in range(n_tensor):
        part = hidden[j]
        at = slice(j * units, (j + 1) * units)
        logits = logits + jnp.dot(part, head_ref[at, :], preferred_element_type=F32)
        value = value + jnp.sum(part.astype(F32) * critic_ref[:, at].astype(F32), axis=1, keepdims=True)
    peak = jnp.max(logits, axis=1, keepdims=True)
    logp = logits - (peak + jnp.log(jnp.sum(jnp.exp(logits - peak), axis=1, keepdims=True)))
    packed = jnp.concatenate([logp, value, jnp.zeros((places, 128 - actions - 1), F32)], axis=1)
    answers[...] = packed.reshape(peers, per, 128)
    returned[row] = answers[row]

    def reply(k):
        return copy(answers.at[lax.rem(row + k, peers)], returned.at[row], b_send.at[k], b_recv.at[k], to_row(k))

    for k in range(1, peers):
        reply(k).start()
    for k in range(1, peers):
        origin = lax.rem(row + peers - k, peers)
        copy(returned.at[origin], returned.at[origin], b_send.at[k], b_recv.at[k], to_row(k)).wait_recv()
    result = jnp.dot(
        hot, returned[...].reshape(places, 128), preferred_element_type=F32, precision=lax.Precision.HIGHEST
    )
    lane = lax.broadcasted_iota(jnp.int32, (rollouts, STEPS), 1)
    all_values = jnp.zeros((rollouts, STEPS), F32)
    for s in range(STEPS):
        now = result[s * rollouts : (s + 1) * rollouts]
        logp_ref[:, s, :] = now[:, :actions]
        all_values = jnp.where(lane == s, now[:, actions : actions + 1], all_values)
    value_ref[...] = all_values
    for k in range(1, peers):
        route(k).wait_send()
        reply(k).wait_send()
    for k in range(1, n_tensor):
        to_units(k).wait_send()
        share(k).wait_send()


def shards(
    frame,
    cache,
    actions,
    owners,
    attn_gain,
    w_query,
    w_keyval,
    w_out,
    action_table,
    policy_in,
    policy_mid,
    policy_head,
    policy_value,
):
    n_tensor = lax.axis_size("tp")
    peers = lax.axis_size("row")
    n_z = n_tensor // 2
    rollouts, _, width = frame.shape
    half = width // 2
    n_rows = n_tensor * rollouts
    n_query = w_query.shape[1]
    n_fresh = w_keyval.shape[1]
    wide = n_query + n_fresh
    cached = cache.shape[2]
    bands = n_rows * 2 * (n_query // HD)
    vmem = pl.BlockSpec(memory_space=pltpu.VMEM)
    dma = pltpu.SemaphoreType.DMA
    latents, rows = pl.pallas_call(
        functools.partial(world_kernel, n_z),
        out_shape=(
            jax.ShapeDtypeStruct((rollouts, width), BF16),
            jax.ShapeDtypeStruct((STEPS, 2 * rollouts, half), BF16),
        ),
        in_specs=[vmem] * 8,
        out_specs=(vmem, vmem),
        scratch_shapes=[
            pltpu.VMEM((rollouts, width), F32),
            pltpu.VMEM((STEPS, n_tensor, 16, half), BF16),
            pltpu.VMEM((STEPS, n_rows, wide), BF16),
            pltpu.VMEM((STEPS, n_rows, wide), BF16),
            pltpu.VMEM((rollouts, 128, HD), BF16),
            pltpu.VMEM((rollouts, 128, HD), BF16),
            pltpu.VMEM((bands, cached + 128), F32),
            pltpu.VMEM((bands, cached + 128), BF16),
            pltpu.VMEM((n_rows, n_query), F32),
            pltpu.VMEM((STEPS, n_rows, wide), BF16),
            pltpu.VMEM((STEPS, n_rows, wide), BF16),
            pltpu.VMEM((n_tensor, 16, half), BF16),
            pltpu.VMEM((STEPS, n_z, 16, half), BF16),
            pltpu.VMEM((n_z, 16, half), BF16),
            pltpu.VMEM((STEPS, n_z, 16, half), BF16),
        ]
        + [dma((STEPS, n_z))] * 5
        + [dma((STEPS, 2))]
        + [dma((STEPS,))] * 4
        + [dma((STEPS, n_z))] * 4,
        compiler_params=pltpu.CompilerParams(
            collective_id=0, has_side_effects=True, vmem_limit_bytes=VMEM_LIMIT
        ),
        name="world",
    )(
        frame.reshape(rollouts, width),
        actions,
        attn_gain.reshape(1, width),
        action_table,
        cache,
        w_query,
        w_keyval,
        w_out,
    )
    n_actions = policy_head.shape[2]
    units = policy_mid.shape[2] // n_tensor
    places = peers * STEPS * CAP
    log_probs, values = pl.pallas_call(
        functools.partial(policy_kernel, peers, n_tensor),
        out_shape=(
            jax.ShapeDtypeStruct((rollouts, STEPS, n_actions), F32),
            jax.ShapeDtypeStruct((rollouts, STEPS), F32),
        ),
        in_specs=[vmem] * 6,
        out_specs=(vmem, vmem),
        scratch_shapes=[
            pltpu.VMEM((peers, 16, half), BF16),
            pltpu.VMEM((peers, 16, half), BF16),
            pltpu.VMEM((n_tensor, places, units), BF16),
            pltpu.VMEM((n_tensor, places, units), BF16),
            pltpu.VMEM((n_tensor, places, units), BF16),
            pltpu.VMEM((peers, STEPS * CAP, 128), F32),
            pltpu.VMEM((peers, STEPS * CAP, 128), F32),
        ]
        + [dma((peers,))] * 2
        + [dma((n_tensor,))] * 4
        + [dma((peers,))] * 2,
        compiler_params=pltpu.CompilerParams(
            collective_id=1, has_side_effects=True, vmem_limit_bytes=VMEM_LIMIT
        ),
        name="policies",
    )(rows, owners, policy_in, policy_mid, policy_head.reshape(policy_head.shape[1:]), policy_value)
    return (latents.reshape(frame.shape), log_probs, values)


def solution(mesh):
    placed = (
        P(("grp", "row"), "tp", None),
        P(("grp", "row"), "tp", None, None),
        P(("grp", "row"), None),
        P(("grp", "row"), None),
        P(),
        P(None, "tp"),
        P(None, "tp"),
        P("tp", None),
        P(),
        P("row", None, "tp"),
        P("row", "tp", None),
        P("row", None, None),
        P("row", None),
    )
    return jax.shard_map(
        shards,
        mesh=mesh,
        in_specs=placed,
        out_specs=(
            P(("grp", "row"), "tp", None),
            P(("grp", "row"), None, None),
            P(("grp", "row"), None),
        ),
        check_vma=False,
    )
```

time: 1670 us -> 314 us (0.19)
  waiting for transfers between devices: 1420 us -> 0 us
  Pallas kernels: 0 us -> 306 us
  starting transfers between devices: 101 us -> 0 us
  matrix products: 50.7 us -> 0 us
  other arithmetic: 33.6 us -> 0 us
  local copies, waits for them, and re-layouts: 39.9 us -> 7.01 us
    reduce_scatter x4 -> x0, waiting for transfers between devices: 810 us -> none  [shards(): reduced = lax.psum_scatter(terms, 'tp', scatter_dimension=1, tiled=True)]
    all_gather x5 -> x0, waiting for transfers between devices: 364 us -> none  [the longest x4 286 us: shards(): world_gathered = lax.all_gather(updated, 'tp', axis=1, tiled=True)]
    pallas_call x0 -> x2, Pallas kernels: none -> 306 us  [the longest x1 266 us: shards(): pl.pallas_call(functools.partial(world_kernel, n_z), out_shape=(jax.Shape...]
    psum x1 -> x0, waiting for transfers between devices: 150 us -> none  [decide(): hidden = jax.nn.silu(lax.psum(partial_hidden, 'tp')).astype(jnp.bfloat16)]
    all_to_all x12 -> x0, starting transfers between devices: 61.6 us -> none  [the longest x4 21.9 us: act(): lax.all_to_all(outgoing, 'row', split_axis=0, concat_axis=0, tiled=True)]
    dot_general x56 -> x0, matrix products: 50.7 us -> none  [the longest x4 10.7 us: shards(): terms = jnp.dot(attended, w_out, preferred_element_type=jnp.float32)]
    ppermute x20 -> x0, waiting for transfers between devices: 45.3 us -> none  [swapped(): lax.ppermute(shard, axis, [(i, i ^ 1 << apart) for i in range(lax.axis_si...]
    all_to_all x12 -> x0, waiting for transfers between devices: 44.2 us -> none  [the longest x4 17.3 us: act(): lax.all_to_all(logp, 'row', split_axis=0, concat_axis=0, tiled=True)]
  transfers between devices with their start and end apart: 42 -> 0, of which waited for: 37 -> 0; matrix products, arithmetic and copies ran while one was open for 4% -> 0% of each run, Pallas kernels for 0% -> 0%
where the time goes in v1:
time: 314 us; the launch traced here: 313 us
  Pallas kernels  306 us (97%)
  local copies, waits for them, and re-layouts  7.01 us (2%)
    pallas_call x1, Pallas kernels, shards(): pl.pallas_call(functools.partial(world_kernel, n_z), out_shape=(jax.Shape...  266 us
    pallas_call x1, Pallas kernels, shards(): pl.pallas_call(functools.partial(policy_kernel, peers, n_tensor), out_sha...  39.8 us
    unnamed x10, local copies, waits for them, and re-layouts  7.01 us

profile of v1, /device:TPU:8, one launch (start us, length us, event | category | flops | bytes accessed | tf_op | source)
XLA Modules:
  0.0 313.4 jit_solution(7637246445799678445)
XLA Ops:
  0.6 1.3 copy.16.actions_ref
  2.0 1.3 copy.18.owners_ref
  3.3 0.0 copy-start
  3.3 265.9 %world.1 = (bf16[8,5120]{1,0:T(8,128)(2,1)}, bf16[4,16,2560]{2,1,0:T(8,128)(2,1)}) custom-call(bf16[8,5120]{1,0:T(8,128)(2,1)} %bitcast.5, s32[8,4]{1,0:T(8,128)} %copy.16.actions_ref, f32[1,5120]{1,0:T(1,128)} %bitcast.7, bf16[18,5120]{1,0:T(8,128)(2,1)} %table_ref.1, bf16[8,1,512,256]{3,2,1,0:T(8,128)(2,1)} %cache_ref.1, bf16[5120,256]{1,0:T(8,128)(2,1)} %wq_ref.1, ...), custom_call_target="tpu_custom_call" | custom-call | tf_op jit(solution)/shard_map/world/pallas_call | solution.py:509
  269.2 0.0 copy-start.1
  269.2 0.0 copy-done
  269.2 1.0 copy.17
  270.3 39.8 %policies.1 = (f32[8,4,18]{2,1,0:T(4,128)}, f32[8,4]{1,0:T(8,128)}) custom-call(bf16[4,16,2560]{2,1,0:T(8,128)(2,1)} %get-tuple-element.8.rows_ref, s32[8,1]{1,0:T(8,128)} %copy.18.owners_ref, bf16[1,5120,128]{2,1,0:T(8,128)(2,1)} %pin_ref.1, bf16[1,128,2048]{2,1,0:T(8,128)(2,1)} %pmid_ref.1, bf16[2048,18]{1,0:T(8,128)(2,1)} %bitcast.4, ...), custom_call_target="tpu_custom_call" | custom-call | tf_op jit(solution)/shard_map/policies/pallas_call | solution.py:555
  310.1 1.3 copy.19
  311.4 0.0 copy-done.1
  311.4 0.6 copy.22
  312.1 1.3 copy.23
Async XLA Ops:
  3.3 265.9 %copy-start = (bf16[1,2048,18]{1,2,0:T(8,128)(2,1)S(1)}, bf16[1,2048,18]{1,2,0:T(8,128)(2,1)}, u32[]{:S(2)}) copy-start(bf16[1,2048,18]{1,2,0:T(8,128)(2,1)} %param.24) | copy-start | bytes 221188
  269.2 42.2 %copy-start.1 = (bf16[8,5120]{1,0:T(8,128)(2,1)S(1)}, bf16[8,5120]{1,0:T(8,128)(2,1)}, u32[]{:S(2)}) copy-start(bf16[8,5120]{1,0:T(8,128)(2,1)} %get-tuple-element.7) | copy-start | bytes 245764

commit v2 on v1

v2 whole, which is shorter than its diff:
```python
import functools

import jax
import jax.numpy as jnp
from jax import lax
from jax.experimental import pallas as pl
from jax.experimental.pallas import tpu as pltpu
from jax.sharding import PartitionSpec as P

HD = 128
STEPS = 4
CAP = 2
EPS = 1e-05
MESH = pl.DeviceIdType.MESH
F32 = jnp.float32
BF16 = jnp.bfloat16
VMEM_LIMIT = 56 << 20


def rms_rows(values):
    return values * lax.rsqrt(jnp.mean(values * values, axis=-1, keepdims=True) + EPS)


def folded(rows):
    half = rows.shape[1] // 2
    return jnp.concatenate([rows[:, :half], rows[:, half:]], axis=0)


PAIR_COLUMNS = 512
FAR = {False: {1: 0, -1: 0, 2: 0, -2: 0, 3: 2, -3: -2, 4: 2}, True: {1: 0, -1: 0, 2: 0, -2: 0, 3: 2, -3: -2, -4: -2}}


def due(tree, k):
    return 0.0 if k == 0 else due(tree, tree[k]) + 2.0 + 0.8 * abs(k - tree[k])


def below(tree, k):
    return sorted([c for c in tree if tree[c] == k], key=lambda c: abs(c - k))


def halves(product, half, width):
    return product.reshape(-1, 2, 8, width)[:, half].reshape(-1, width)


def fold_dot(first, second, weight):
    half = weight.shape[0] // 2
    columns = weight.shape[1]
    cut = first.shape[1]
    left = jnp.dot(first, weight[:cut], preferred_element_type=F32)
    left = left + jnp.dot(second, weight[cut:half], preferred_element_type=F32)
    right = jnp.dot(first, weight[half : half + cut], preferred_element_type=F32)
    right = right + jnp.dot(second, weight[half + cut :], preferred_element_type=F32)
    return halves(left, 0, columns) + halves(right, 1, columns)


def silu(values):
    return values / (1.0 + jnp.exp(-values))


def kernel(
    n_z,
    peers,
    frame_ref,
    actions_ref,
    owners_ref,
    gain_ref,
    table_ref,
    cache_ref,
    wq_ref,
    wkv_ref,
    wo_ref,
    pin_ref,
    pmid_ref,
    head_ref,
    critic_ref,
    latents_ref,
    logp_ref,
    value_ref,
    state,
    gath_p,
    gath_q,
    qkv,
    qkv_in,
    keys,
    vals,
    scores,
    weights,
    own_o,
    out_o,
    in_o,
    terms_p,
    terms_q,
    tree_p,
    tree_q,
    pair_p,
    pair_q,
    latent_rows,
    outgoing,
    arrived,
    partial,
    partial_in,
    hidden,
    answers,
    returned,
    ag_zs,
    ag_zr,
    ag_ys,
    ag_yr,
    rs_zs,
    rs_zr,
    rs_ys,
    rs_yr,
    q_send,
    q_recv,
    o_send,
    o_recv,
    l_send,
    l_recv,
    a_send,
    a_recv,
    h_send,
    h_recv,
    g_send,
    g_recv,
    b_send,
    b_recv,
):
    tensor = lax.axis_index("tp")
    row = lax.axis_index("row")
    z = tensor // 2
    yh = lax.rem(tensor, 2)
    pair = {"tp": tensor + 1 - 2 * yh}
    rollouts, width = state.shape
    n_tensor = 2 * n_z
    tokens = n_tensor
    n_rows = tokens * rollouts
    cached = cache_ref.shape[2]
    last = n_tensor - 1
    cut = gath_p.shape[3]
    half = width // 2

    def plane(k):
        return lax.rem(z + k + 2 * n_z, n_z)

    def to_plane(k):
        return {"tp": plane(k) * 2 + yh}

    def slot_of(k, other):
        return plane(k) * 2 + (1 - yh if other else yh)

    def to_row(k):
        return {"row": lax.rem(row + k, peers)}

    def to_tensor(k):
        return {"tp": lax.rem(tensor + k, n_tensor)}

    barrier = pltpu.get_barrier_semaphore()
    for k in range(1, n_tensor):
        pl.semaphore_signal(barrier, inc=1, device_id=to_tensor(k), device_id_type=MESH)
    for k in range(1, peers):
        pl.semaphore_signal(barrier, inc=1, device_id=to_row(k), device_id_type=MESH)

    def copy(src, dst, send, recv, target):
        return pltpu.make_async_remote_copy(
            src_ref=src, dst_ref=dst, send_sem=send, recv_sem=recv, device_id=target, device_id_type=MESH
        )

    state[...] = frame_ref[...].astype(F32)
    keys[...] = jnp.zeros_like(keys)
    vals[...] = jnp.zeros_like(vals)
    iota_r = lax.broadcasted_iota(jnp.int32, (n_rows, n_rows), 0)
    iota_c = lax.broadcasted_iota(jnp.int32, (n_rows, n_rows), 1)
    by_rollout = (lax.rem(iota_r, tokens) * rollouts + iota_r // tokens == iota_c).astype(F32).astype(BF16)
    by_token = (lax.rem(iota_c, tokens) * rollouts + iota_c // tokens == iota_r).astype(F32).astype(BF16)

    owner = owners_ref[...]
    hit = (lax.broadcasted_iota(jnp.int32, (rollouts, 128), 1) == owner).astype(F32)
    later = (
        lax.broadcasted_iota(jnp.int32, (rollouts, rollouts), 0)
        > lax.broadcasted_iota(jnp.int32, (rollouts, rollouts), 1)
    ).astype(F32)
    before = jnp.zeros((rollouts, 128), F32)
    for r in range(rollouts):
        before = before + later[:, r : r + 1] * hit[r : r + 1, :]
    place_of = jnp.sum(before * hit, axis=1, keepdims=True)
    eighths = 16 // CAP
    spots = peers * 16
    tn = (((0,), (0,)), ((), ()))
    pl.semaphore_wait(barrier, peers + n_tensor - 2)

    def spread_out(q, k):
        mine = latent_rows.at[q]
        for c in below(FAR[False], k):
            copy(mine, mine, l_send.at[q, c % n_z], l_recv.at[q, 0], to_plane(c - k)).start()
        copy(mine, mine, l_send.at[q, 0], l_recv.at[q, 1], pair).start()

    def spread_sent(q, k):
        mine = latent_rows.at[q]
        for c in below(FAR[False], k):
            copy(mine, mine, l_send.at[q, c % n_z], l_recv.at[q, 0], to_plane(c - k)).wait_send()
        copy(mine, mine, l_send.at[q, 0], l_recv.at[q, 1], pair).wait_send()

    def spread_start(q):
        @pl.when(tensor == last)
        def _():
            spread_out(q, 0)

    def spread_on(q):
        mine = latent_rows.at[q]
        for k in FAR[False]:

            @pl.when(tensor == (last + 2 * k) % n_tensor)
            def _():
                copy(mine, mine, l_send.at[q, 0], l_recv.at[q, 0], pair).wait_recv()
                spread_out(q, k)

        @pl.when(yh == 0)
        def _():
            copy(mine, mine, l_send.at[q, 0], l_recv.at[q, 1], pair).wait_recv()

    def spread_end(q):
        for k in [0] + list(FAR[False]):

            @pl.when(tensor == (last + 2 * k) % n_tensor)
            def _():
                spread_sent(q, k)

    def route(q, k):
        return copy(
            outgoing.at[q, lax.rem(row + k, peers)], arrived.at[q, row], a_send.at[q, k], a_recv.at[q, k], to_row(k)
        )

    def route_start(q):
        wide = half // 4
        i = lax.broadcasted_iota(jnp.int32, (16, spots), 1)
        j = lax.broadcasted_iota(jnp.int32, (16, spots), 0)
        owner2 = jnp.concatenate([owner, owner], axis=0)
        place2 = jnp.concatenate([place_of, place_of], axis=0)
        chosen = (i // 16 == owner2) & (lax.rem(i, CAP).astype(F32) == place2)
        eighth = lax.rem(i // CAP, eighths)
        built = jnp.zeros((spots, wide), F32)
        for quarter in range(4):
            hot = (chosen & (eighth == (j // rollouts) * 4 + quarter)).astype(F32).astype(BF16)
            built = built + lax.dot_general(
                hot, latent_rows[q, :, quarter * wide : (quarter + 1) * wide], tn, preferred_element_type=F32
            )
        outgoing[q] = built.astype(BF16).reshape(peers, 16, wide)
        arrived[q, row] = outgoing[q, row]
        for k in range(1, peers):
            route(q, k).start()

    def to_units(q, k):
        return copy(
            partial.at[q, lax.rem(tensor + k, n_tensor)],
            partial_in.at[q, k],
            h_send.at[q, k],
            h_recv.at[q, k],
            to_tensor(k),
        )

    def inner_start(q):
        for k in range(1, peers):
            origin = arrived.at[q, lax.rem(row + peers - k, peers)]
            copy(origin, origin, a_send.at[q, k], a_recv.at[q, k], to_row(k)).wait_recv()
        wide = half // 4
        rows = arrived[q].reshape(spots, wide)
        n_inner = pin_ref.shape[2]
        at_row = lax.rem(lax.broadcasted_iota(jnp.int32, (spots, n_inner), 0) // CAP, eighths)
        picked = jnp.zeros((spots, n_inner), F32)
        for e in range(eighths):
            product = jnp.dot(rows, pin_ref[0, e * wide : (e + 1) * wide, :], preferred_element_type=F32)
            picked = picked + jnp.where(at_row == e, product, 0.0)
        i = lax.broadcasted_iota(jnp.int32, (16, spots), 1)
        j = lax.broadcasted_iota(jnp.int32, (16, spots), 0)
        gather = ((i // 16 == j // CAP) & (lax.rem(i, CAP) == lax.rem(j, CAP))).astype(F32)
        before_silu = jnp.dot(gather, picked, preferred_element_type=F32, precision=lax.Precision.HIGHEST)
        inner = silu(before_silu).astype(BF16)
        units = partial.shape[3]
        product = jnp.dot(inner, pmid_ref[0], preferred_element_type=F32).astype(BF16)
        for t in range(n_tensor):
            partial[q, t] = product[:, t * units : (t + 1) * units]
        for k in range(1, n_tensor):
            to_units(q, k).start()

    def share(q, k):
        mine = hidden.at[q, tensor]
        return copy(mine, mine, g_send.at[q, k], g_recv.at[q, k], to_tensor(k))

    def hidden_start(q):
        summed = partial[q, tensor].astype(F32)
        for k in range(1, n_tensor):
            to_units(q, k).wait_recv()
            summed = summed + partial_in[q, k].astype(F32)
        hidden[q, tensor] = silu(summed).astype(BF16)
        for k in range(1, n_tensor):
            share(q, k).start()

    def reply(q, k):
        return copy(answers.at[q], returned.at[q, row], b_send.at[q, k], b_recv.at[q, k], to_row(k))

    def heads_start(q):
        for k in range(1, n_tensor):
            origin = hidden.at[q, lax.rem(tensor + n_tensor - k, n_tensor)]
            copy(origin, origin, g_send.at[q, k], g_recv.at[q, k], to_tensor(k)).wait_recv()
        whole = jnp.concatenate([hidden[q, t] for t in range(n_tensor)], axis=1)
        logits = jnp.dot(whole, head_ref[...], preferred_element_type=F32)
        value = jnp.sum(whole.astype(F32) * critic_ref[...].astype(F32), axis=1, keepdims=True)
        peak = jnp.max(logits, axis=1, keepdims=True)
        logp = logits - (peak + jnp.log(jnp.sum(jnp.exp(logits - peak), axis=1, keepdims=True)))
        blank = jnp.zeros((16, 128 - logits.shape[1] - 1), F32)
        answers[q] = jnp.concatenate([logp, value, blank], axis=1)
        returned[q, row] = answers[q]
        for k in range(1, peers):
            reply(q, k).start()

    def policy_end(q):
        for k in range(1, peers):
            origin = returned.at[q, lax.rem(row + peers - k, peers)]
            copy(origin, origin, b_send.at[q, k], b_recv.at[q, k], to_row(k)).wait_recv()
        spread_end(q)
        for k in range(1, peers):
            route(q, k).wait_send()
            reply(q, k).wait_send()
        for k in range(1, n_tensor):
            to_units(q, k).wait_send()
            share(q, k).wait_send()

    def gather(s):
        own, other, front = FAR[False], FAR[True], FAR[False]
        sent = []

        def block(stream, k):
            return (gath_q if stream == 2 else gath_p).at[s, slot_of(-k, stream == 1)]

        def go(ref, send, recv, target):
            moved = copy(ref, ref, send, recv, target)
            moved.start()
            sent.append(moved)

        def spread(stream, tree, k):
            for c in below(tree, k):
                go(block(stream, k), ag_zs.at[s, stream, c % n_z], ag_zr.at[s, stream, c % n_z], to_plane(c - k))

        def pass_on(k):
            go(block(2, k), ag_ys.at[s, k % n_z], ag_yr.at[s, k % n_z], pair)

        go(block(0, 0), ag_ys.at[s, n_z], ag_yr.at[s, n_z], pair)
        spread(2, front, 0)
        pass_on(0)
        spread(0, own, 0)
        events = [(due(front, k), 2, k) for k in front] + [(due(own, k), 0, k) for k in own]
        events += [(3.0 + due(other, k), 1, k) for k in [0] + list(other)]
        for _, stream, k in sorted(events):
            ref = block(stream, k)
            if k == 0:
                copy(ref, ref, ag_ys.at[s, n_z], ag_yr.at[s, n_z], pair).wait_recv()
            else:
                copy(ref, ref, ag_zs.at[s, stream, k % n_z], ag_zr.at[s, stream, k % n_z], pair).wait_recv()
            spread(stream, (own, other, front)[stream], k)
            if stream == 2:
                pass_on(k)
        for k in [0] + list(front):
            ref = gath_q.at[s, slot_of(-k, True)]
            copy(ref, ref, ag_ys.at[s, k % n_z], ag_yr.at[s, k % n_z], pair).wait_recv()
        return sent

    def scatter(s, meanwhile):
        trees = (FAR[False], FAR[True], FAR[False])
        sent = []

        def go(src, dst, send, recv, target):
            moved = copy(src, dst, send, recv, target)
            moved.start()
            sent.append(moved)

        for k in sorted(trees[2], key=lambda k: -due(trees[2], k)) + [0]:
            go(
                terms_q.at[slot_of(-k, True)],
                pair_q.at[s, k % n_z],
                rs_ys.at[s, k % n_z],
                rs_yr.at[s, k % n_z],
                pair,
            )
        deepest = max(due(trees[0], k) for k in trees[0])
        events = []
        for stream, offset in ((0, 1.0), (1, -0.1), (2, 3.0)):
            events += [(offset + deepest - due(trees[stream], k), stream, k) for k in [0] + list(trees[stream])]
        ends = {}
        for number, (_, stream, k) in enumerate(sorted(events)):
            if number == len(events) // 2:
                meanwhile()
            tree = trees[stream]
            terms = terms_q if stream == 2 else terms_p
            slot = slot_of(-k, stream == 1)

            def landing(c):
                return tree_q.at[s, c % n_z] if stream == 2 else tree_p.at[s, stream, c % n_z]

            total = None
            children = below(tree, k)
            if stream == 2 or children or k == 0:
                total = terms[slot].astype(F32)
            if stream == 2:
                ref = pair_q.at[s, k % n_z]
                copy(ref, ref, rs_ys.at[s, k % n_z], rs_yr.at[s, k % n_z], pair).wait_recv()
                total = total + pair_q[s, k % n_z].astype(F32)
            for c in children:
                ref = landing(c)
                copy(ref, ref, rs_zs.at[s, stream, c % n_z], rs_zr.at[s, stream, c % n_z], pair).wait_recv()
                total = total + ref[...].astype(F32)
            if k:
                if total is not None:
                    terms[slot] = total.astype(BF16)
                go(
                    terms.at[slot],
                    landing(k),
                    rs_zs.at[s, stream, k % n_z],
                    rs_zr.at[s, stream, k % n_z],
                    to_plane(tree[k] - k),
                )
            elif stream == 1:
                terms[slot] = total.astype(BF16)
                go(terms.at[slot], pair_p.at[s], rs_ys.at[s, n_z], rs_yr.at[s, n_z], pair)
            else:
                ends[stream] = total
        ref = pair_p.at[s]
        copy(ref, ref, rs_ys.at[s, n_z], rs_yr.at[s, n_z], pair).wait_recv()
        first = ends[0] + pair_p[s].astype(F32)
        both = jnp.concatenate([first, ends[2]], axis=1)
        return jnp.concatenate([both[:rollouts], both[rollouts:]], axis=1), sent

    def step(s, carry):
        picked = jnp.sum(
            jnp.where(lax.broadcasted_iota(jnp.int32, actions_ref.shape, 1) == s, actions_ref[...], 0),
            axis=1,
            keepdims=True,
        )
        code = (lax.broadcasted_iota(jnp.int32, (rollouts, table_ref.shape[0]), 1) == picked).astype(F32).astype(BF16)
        embed = jnp.dot(code, table_ref[...], preferred_element_type=F32)
        inputs = (state[...] + embed).astype(BF16).astype(F32)
        state[...] = inputs
        normed = folded(rms_rows(inputs) * gain_ref[...]).astype(BF16)
        gath_p[s, tensor] = normed[:, :cut]
        gath_q[s, tensor] = normed[:, cut:]
        gathered = gather(s)

        first = gath_p[s].reshape(n_tensor * 16, cut)
        second = gath_q[s].reshape(n_tensor * 16, half - cut)
        query = (fold_dot(first, second, wq_ref) * HD ** (-0.5)).astype(BF16)
        keyval = fold_dot(first, second, wkv_ref).astype(BF16)
        n_query = query.shape[1]
        qkv[s, :, :n_query] = jnp.dot(by_rollout, query, preferred_element_type=F32).astype(BF16)
        qkv[s, :, n_query:] = jnp.dot(by_rollout, keyval, preferred_element_type=F32).astype(BF16)
        swap = copy(qkv.at[s], qkv_in.at[s], q_send.at[s], q_recv.at[s], pair)
        swap.start()

        @pl.when(s > 0)
        def _():
            spread_on(s - 1)
            route_start(s - 1)

        for moved in gathered:
            moved.wait_send()
        swap.wait()

        own_kv = qkv[s, :, n_query:].astype(F32)
        other_kv = qkv_in[s, :, n_query:].astype(F32)
        new_key = jnp.where(yh == 0, own_kv, other_kv).astype(BF16)
        new_val = jnp.where(yh == 0, other_kv, own_kv).astype(BF16)
        place = pl.ds(pl.multiple_of(s * tokens, tokens), tokens)
        heads = n_query // HD
        per = 2 * heads * tokens
        nt = (((1,), (1,)), ((), ()))
        for r in range(rollouts):
            rows = slice(r * tokens, (r + 1) * tokens)
            keys[r, place, :] = new_key[rows]
            vals[r, place, :] = new_val[rows]
            parts = [qkv[s, rows, h * HD : (h + 1) * HD] for h in range(heads)]
            parts += [qkv_in[s, rows, h * HD : (h + 1) * HD] for h in range(heads)]
            grouped = jnp.concatenate(parts, axis=0)
            band = slice(r * per, (r + 1) * per)
            scores[band, :cached] = lax.dot_general(
                grouped, cache_ref[r, 0, :, :HD], nt, preferred_element_type=F32
            )
            scores[band, cached:] = lax.dot_general(grouped, keys[r], nt, preferred_element_type=F32)
        fresh = scores[:, cached:]
        key_pos = lax.broadcasted_iota(jnp.int32, fresh.shape, 1)
        query_pos = lax.rem(lax.broadcasted_iota(jnp.int32, fresh.shape, 0), tokens)
        allowed = (key_pos <= s * tokens + query_pos) & (yh == 0)
        fresh = jnp.where(allowed, fresh, -jnp.inf)
        old = scores[:, :cached]
        top = jnp.maximum(jnp.max(old, axis=1, keepdims=True), jnp.max(fresh, axis=1, keepdims=True))
        old = jnp.exp(old - top)
        fresh = jnp.exp(fresh - top)
        total = jnp.sum(old, axis=1, keepdims=True) + jnp.sum(fresh, axis=1, keepdims=True)
        weights[:, :cached] = old.astype(BF16)
        weights[:, cached:] = fresh.astype(BF16)
        inverse = 1.0 / total
        lane = lax.broadcasted_iota(jnp.int32, (tokens, HD), 1)
        for r in range(rollouts):
            rows = slice(r * tokens, (r + 1) * tokens)
            band = slice(r * per, (r + 1) * per)
            summed = jnp.dot(weights[band, :cached], cache_ref[r, 0, :, HD:], preferred_element_type=F32)
            summed = summed + jnp.dot(weights[band, cached:], vals[r], preferred_element_type=F32)
            summed = summed * inverse[band]
            stats = jnp.zeros((tokens, HD), F32)
            for h in range(heads):
                own_o[rows, h * HD : (h + 1) * HD] = summed[h * tokens : (h + 1) * tokens]
                far = slice((heads + h) * tokens, (heads + h + 1) * tokens)
                out_o[s, rows, h * HD : (h + 1) * HD] = summed[far].astype(BF16)
                left = top[band][far]
                for piece in range(3):
                    term = left.astype(BF16).astype(F32)
                    left = left - term
                    stats = jnp.where(lane == 8 * h + piece, term, stats)
                left = total[band][far]
                for piece in range(3):
                    term = left.astype(BF16).astype(F32)
                    left = left - term
                    stats = jnp.where(lane == 8 * h + 3 + piece, term, stats)
            out_o[s, rows, n_query:] = stats.astype(BF16)
        swap = copy(out_o.at[s], in_o.at[s], o_send.at[s], o_recv.at[s], pair)
        swap.start()

        @pl.when(s > 0)
        def _():
            inner_start(s - 1)

        swap.wait()

        stats = in_o[s, :, n_query:].astype(F32)
        top4 = top.reshape(rollouts, 2 * heads, tokens, 1)
        total4 = total.reshape(rollouts, 2 * heads, tokens, 1)
        joined = []
        for h in range(heads):
            pick = [stats[:, 8 * h + i : 8 * h + i + 1] for i in range(6)]
            far_top = pick[0] + pick[1] + pick[2]
            far_total = pick[3] + pick[4] + pick[5]
            near_top = top4[:, h].reshape(n_rows, 1)
            near_total = total4[:, h].reshape(n_rows, 1)
            peak = jnp.maximum(near_top, far_top)
            near = near_total * jnp.exp(near_top - peak)
            far = far_total * jnp.exp(far_top - peak)
            both = 1.0 / (near + far)
            cols = slice(h * HD, (h + 1) * HD)
            joined.append(own_o[:, cols] * (near * both) + in_o[s, :, cols].astype(F32) * (far * both))
        attended = jnp.concatenate(joined, axis=1).astype(BF16)
        attended = jnp.dot(by_token, attended, preferred_element_type=F32).astype(BF16)

        tile = 512 if half % 512 == 0 else HD
        for j in range(half // tile):
            at = slice(j * tile, (j + 1) * tile)
            also = slice(half + j * tile, half + (j + 1) * tile)
            left = jnp.dot(attended, wo_ref[:, at], preferred_element_type=F32).reshape(tokens, rollouts, tile)
            right = jnp.dot(attended, wo_ref[:, also], preferred_element_type=F32).reshape(tokens, rollouts, tile)
            part = jnp.concatenate([left, right], axis=1).astype(BF16)
            if j * tile < cut:
                terms_p[:, :, at] = part
            else:
                terms_q[:, :, j * tile - cut : (j + 1) * tile - cut] = part

        def meanwhile():
            @pl.when(s > 0)
            def _():
                hidden_start(s - 1)

        reduced, sent = scatter(s, meanwhile)
        updated = (state[...] + reduced).astype(BF16).astype(F32)
        state[...] = updated

        @pl.when(tensor == last)
        def _():
            latent_rows[s] = folded(rms_rows(updated)).astype(BF16)

        spread_start(s)
        for moved in sent:
            moved.wait_send()

        @pl.when(s > 0)
        def _():
            heads_start(s - 1)

        return carry

    lax.fori_loop(0, STEPS, step, 0)
    latents_ref[...] = state[...].astype(BF16)
    final = STEPS - 1
    spread_on(final)
    route_start(final)
    inner_start(final)
    hidden_start(final)
    heads_start(final)
    i = lax.broadcasted_iota(jnp.int32, (rollouts, spots), 1)
    mine = (i // 16 == owner) & (lax.rem(i, CAP).astype(F32) == place_of) & (lax.rem(i // CAP, eighths) == row)
    mine = mine.astype(F32)
    lane = lax.broadcasted_iota(jnp.int32, (rollouts, STEPS), 1)
    all_values = jnp.zeros((rollouts, STEPS), F32)
    n_actions = head_ref.shape[1]
    for q in range(STEPS):
        policy_end(q)
        now = jnp.dot(
            mine, returned[q].reshape(spots, 128), preferred_element_type=F32, precision=lax.Precision.HIGHEST
        )
        logp_ref[:, q, :] = now[:, :n_actions]
        all_values = jnp.where(lane == q, now[:, n_actions : n_actions + 1], all_values)
    value_ref[...] = all_values


def shards(
    frame,
    cache,
    actions,
    owners,
    attn_gain,
    w_query,
    w_keyval,
    w_out,
    action_table,
    policy_in,
    policy_mid,
    policy_head,
    policy_value,
):
    n_tensor = lax.axis_size("tp")
    peers = lax.axis_size("row")
    n_z = n_tensor // 2
    rollouts, _, width = frame.shape
    half = width // 2
    n_rows = n_tensor * rollouts
    n_query = w_query.shape[1]
    wide = n_query + w_keyval.shape[1]
    cached = cache.shape[2]
    bands = n_rows * 2 * (n_query // HD)
    units = policy_mid.shape[2] // n_tensor
    cut = PAIR_COLUMNS
    vmem = pl.BlockSpec(memory_space=pltpu.VMEM)
    dma = pltpu.SemaphoreType.DMA
    latents, log_probs, values = pl.pallas_call(
        functools.partial(kernel, n_z, peers),
        out_shape=(
            jax.ShapeDtypeStruct((rollouts, width), BF16),
            jax.ShapeDtypeStruct((rollouts, STEPS, policy_head.shape[2]), F32),
            jax.ShapeDtypeStruct((rollouts, STEPS), F32),
        ),
        in_specs=[vmem] * 13,
        out_specs=(vmem,) * 3,
        scratch_shapes=[
            pltpu.VMEM((rollouts, width), F32),
            pltpu.VMEM((STEPS, n_tensor, 16, cut), BF16),
            pltpu.VMEM((STEPS, n_tensor, 16, half - cut), BF16),
            pltpu.VMEM((STEPS, n_rows, wide), BF16),
            pltpu.VMEM((STEPS, n_rows, wide), BF16),
            pltpu.VMEM((rollouts, 128, HD), BF16),
            pltpu.VMEM((rollouts, 128, HD), BF16),
            pltpu.VMEM((bands, cached + 128), F32),
            pltpu.VMEM((bands, cached + 128), BF16),
            pltpu.VMEM((n_rows, n_query), F32),
            pltpu.VMEM((STEPS, n_rows, wide), BF16),
            pltpu.VMEM((STEPS, n_rows, wide), BF16),
            pltpu.VMEM((n_tensor, 16, cut), BF16),
            pltpu.VMEM((n_tensor, 16, half - cut), BF16),
            pltpu.VMEM((STEPS, 2, n_z, 16, cut), BF16),
            pltpu.VMEM((STEPS, n_z, 16, half - cut), BF16),
            pltpu.VMEM((STEPS, 16, cut), BF16),
            pltpu.VMEM((STEPS, n_z, 16, half - cut), BF16),
            pltpu.VMEM((STEPS, 16, half), BF16),
            pltpu.VMEM((STEPS, peers, 16, half // 4), BF16),
            pltpu.VMEM((STEPS, peers, 16, half // 4), BF16),
            pltpu.VMEM((STEPS, n_tensor, 16, units), BF16),
            pltpu.VMEM((STEPS, n_tensor, 16, units), BF16),
            pltpu.VMEM((STEPS, n_tensor, 16, units), BF16),
            pltpu.VMEM((STEPS, 16, 128), F32),
            pltpu.VMEM((STEPS, peers, 16, 128), F32),
        ]
        + [dma((STEPS, 3, n_z))] * 2
        + [dma((STEPS, n_z + 1))] * 2
        + [dma((STEPS, 3, n_z))] * 2
        + [dma((STEPS, n_z + 1))] * 2
        + [dma((STEPS,))] * 4
        + [dma((STEPS, n_z)), dma((STEPS, 2))]
        + [dma((STEPS, peers))] * 2
        + [dma((STEPS, n_tensor))] * 4
        + [dma((STEPS, peers))] * 2,
        compiler_params=pltpu.CompilerParams(
            collective_id=0, has_side_effects=True, vmem_limit_bytes=VMEM_LIMIT
        ),
        name="imagine",
    )(
        frame.reshape(rollouts, width),
        actions,
        owners,
        attn_gain.reshape(1, width),
        action_table,
        cache,
        w_query,
        w_keyval,
        w_out,
        policy_in,
        policy_mid,
        policy_head.reshape(policy_head.shape[1:]),
        policy_value,
    )
    return (latents.reshape(frame.shape), log_probs, values)


def solution(mesh):
    placed = (
        P(("grp", "row"), "tp", None),
        P(("grp", "row"), "tp", None, None),
        P(("grp", "row"), None),
        P(("grp", "row"), None),
        P(),
        P(None, "tp"),
        P(None, "tp"),
        P("tp", None),
        P(),
        P("row", None, "tp"),
        P("row", "tp", None),
        P("row", None, None),
        P("row", None),
    )
    return jax.shard_map(
        shards,
        mesh=mesh,
        in_specs=placed,
        out_specs=(
            P(("grp", "row"), "tp", None),
            P(("grp", "row"), None, None),
            P(("grp", "row"), None),
        ),
        check_vma=False,
    )
```

time: 314 us -> 277 us (0.88)
  Pallas kernels: 306 us -> 267 us
    pallas_call x2 -> x1, Pallas kernels: 306 us -> 267 us  [shards(): pl.pallas_call(functools.partial(kernel, n_z, peers), out_shape=(jax.Shap...]
    unnamed x10 -> x6, local copies, waits for them, and re-layouts: 7.01 us -> 8.77 us
where the time goes in v2:
time: 277 us
  Pallas kernels  267 us (96%)
  local copies, waits for them, and re-layouts  8.77 us (3%)
    pallas_call x1, Pallas kernels, shards(): pl.pallas_call(functools.partial(kernel, n_z, peers), out_shape=(jax.Shap...  267 us
    unnamed x6, local copies, waits for them, and re-layouts  8.77 us

profile of v2, /device:TPU:8, one launch (start us, length us, event | category | flops | bytes accessed | tf_op | source)
XLA Modules:
  0.0 276.5 jit_solution(9668048749638087396)
XLA Ops:
  0.6 1.3 copy.17.actions_ref
  2.0 1.3 copy.18.owners_ref
  3.3 1.9 copy.16
  5.2 267.1 %imagine.1 = (bf16[8,5120]{1,0:T(8,128)(2,1)}, f32[8,4,18]{2,1,0:T(4,128)}, f32[8,4]{1,0:T(8,128)}) custom-call(bf16[8,5120]{1,0:T(8,128)(2,1)} %bitcast.6, s32[8,4]{1,0:T(8,128)} %copy.17.actions_ref, s32[8,1]{1,0:T(8,128)} %copy.18.owners_ref, f32[1,5120]{1,0:T(1,128)} %bitcast.7, bf16[18,5120]{1,0:T(8,128)(2,1)} %table_ref.1, ...), custom_call_target="tpu_custom_call" | custom-call | tf_op jit(solution)/shard_map/imagine/pallas_call | solution.py:638
  272.3 1.3 copy.19
  273.7 1.5 copy.22
  275.2 1.3 copy.23

commit v3 on v2

--- a/solution.py
+++ b/solution.py
@@ -65,17 +65,24 @@
     owners_ref,
     gain_ref,
     table_ref,
+    cache_hbm,
+    wq_hbm,
+    wkv_hbm,
+    wo_hbm,
+    pin_hbm,
+    pmid_hbm,
+    head_ref,
+    critic_ref,
+    latents_ref,
+    logp_ref,
+    value_ref,
     cache_ref,
     wq_ref,
     wkv_ref,
     wo_ref,
     pin_ref,
     pmid_ref,
-    head_ref,
-    critic_ref,
-    latents_ref,
-    logp_ref,
-    value_ref,
+    embed,
     state,
     gath_p,
     gath_q,
@@ -124,7 +131,23 @@
     g_recv,
     b_send,
     b_recv,
+    loaded,
 ):
+    loads = [
+        pltpu.make_async_copy(src, dst, loaded.at[i])
+        for i, (src, dst) in enumerate(
+            (
+                (wq_hbm, wq_ref),
+                (wkv_hbm, wkv_ref),
+                (cache_hbm, cache_ref),
+                (wo_hbm, wo_ref),
+                (pin_hbm, pin_ref),
+                (pmid_hbm, pmid_ref),
+            )
+        )
+    ]
+    for load in loads:
+        load.start()
     tensor = lax.axis_index("tp")
     row = lax.axis_index("row")
     z = tensor // 2
@@ -173,7 +196,10 @@
     by_rollout = (lax.rem(iota_r, tokens) * rollouts + iota_r // tokens == iota_c).astype(F32).astype(BF16)
     by_token = (lax.rem(iota_c, tokens) * rollouts + iota_c // tokens == iota_r).astype(F32).astype(BF16)
 
-    owner = owners_ref[...]
+    eye = lax.broadcasted_iota(jnp.int32, (rollouts, rollouts), 0) == lax.broadcasted_iota(
+        jnp.int32, (rollouts, rollouts), 1
+    )
+    owner = jnp.sum(jnp.where(eye, owners_ref[...], 0), axis=1, keepdims=True)
     hit = (lax.broadcasted_iota(jnp.int32, (rollouts, 128), 1) == owner).astype(F32)
     later = (
         lax.broadcasted_iota(jnp.int32, (rollouts, rollouts), 0)
@@ -186,6 +212,7 @@
     eighths = 16 // CAP
     spots = peers * 16
     tn = (((0,), (0,)), ((), ()))
+    nt = (((1,), (1,)), ((), ()))
     pl.semaphore_wait(barrier, peers + n_tensor - 2)
 
     def spread_out(q, k):
@@ -303,7 +330,7 @@
             origin = hidden.at[q, lax.rem(tensor + n_tensor - k, n_tensor)]
             copy(origin, origin, g_send.at[q, k], g_recv.at[q, k], to_tensor(k)).wait_recv()
         whole = jnp.concatenate([hidden[q, t] for t in range(n_tensor)], axis=1)
-        logits = jnp.dot(whole, head_ref[...], preferred_element_type=F32)
+        logits = lax.dot_general(whole, head_ref[...], nt, preferred_element_type=F32)
         value = jnp.sum(whole.astype(F32) * critic_ref[...].astype(F32), axis=1, keepdims=True)
         peak = jnp.max(logits, axis=1, keepdims=True)
         logp = logits - (peak + jnp.log(jnp.sum(jnp.exp(logits - peak), axis=1, keepdims=True)))
@@ -364,7 +391,7 @@
             copy(ref, ref, ag_ys.at[s, k % n_z], ag_yr.at[s, k % n_z], pair).wait_recv()
         return sent
 
-    def scatter(s, meanwhile):
+    def scatter(s, hooks):
         trees = (FAR[False], FAR[True], FAR[False])
         sent = []
 
@@ -387,8 +414,8 @@
             events += [(offset + deepest - due(trees[stream], k), stream, k) for k in [0] + list(trees[stream])]
         ends = {}
         for number, (_, stream, k) in enumerate(sorted(events)):
-            if number == len(events) // 2:
-                meanwhile()
+            if number in (len(events) // 2, len(events) * 7 // 8):
+                hooks.pop(0)()
             tree = trees[stream]
             terms = terms_q if stream == 2 else terms_p
             slot = slot_of(-k, stream == 1)
@@ -429,20 +456,26 @@
         both = jnp.concatenate([first, ends[2]], axis=1)
         return jnp.concatenate([both[:rollouts], both[rollouts:]], axis=1), sent
 
+    def embed_actions(s):
+        at_step = lax.broadcasted_iota(jnp.int32, actions_ref.shape, 0) == s
+        picked = jnp.sum(jnp.where(at_step, actions_ref[...], 0), axis=0, keepdims=True)
+        code = lax.broadcasted_iota(jnp.int32, (table_ref.shape[0], rollouts), 0) == picked
+        embed[...] = lax.dot_general(
+            code.astype(F32).astype(BF16), table_ref[...], tn, preferred_element_type=F32
+        )
+
     def step(s, carry):
-        picked = jnp.sum(
-            jnp.where(lax.broadcasted_iota(jnp.int32, actions_ref.shape, 1) == s, actions_ref[...], 0),
-            axis=1,
-            keepdims=True,
-        )
-        code = (lax.broadcasted_iota(jnp.int32, (rollouts, table_ref.shape[0]), 1) == picked).astype(F32).astype(BF16)
-        embed = jnp.dot(code, table_ref[...], preferred_element_type=F32)
-        inputs = (state[...] + embed).astype(BF16).astype(F32)
+        inputs = (state[...] + embed[...]).astype(BF16).astype(F32)
         state[...] = inputs
         normed = folded(rms_rows(inputs) * gain_ref[...]).astype(BF16)
         gath_p[s, tensor] = normed[:, :cut]
         gath_q[s, tensor] = normed[:, cut:]
         gathered = gather(s)
+
+        @pl.when(s == 0)
+        def _():
+            for load in loads:
+                load.wait()
 
         first = gath_p[s].reshape(n_tensor * 16, cut)
         second = gath_q[s].reshape(n_tensor * 16, half - cut)
@@ -454,6 +487,29 @@
         swap = copy(qkv.at[s], qkv_in.at[s], q_send.at[s], q_recv.at[s], pair)
         swap.start()
 
+        heads = n_query // HD
+        per = heads * tokens
+
+        def grouped(source, r):
+            rows = slice(r * tokens, (r + 1) * tokens)
+            return jnp.concatenate([source[s, rows, h * HD : (h + 1) * HD] for h in range(heads)], axis=0)
+
+        def band(r):
+            return slice(r * per, (r + 1) * per)
+
+        def score_cached(group, source, r):
+            scores[group, band(r), :cached] = lax.dot_general(
+                grouped(source, r), cache_ref[r, 0, :, :HD], nt, preferred_element_type=F32
+            )
+
+        def score_new(group, source, r):
+            scores[group, band(r), cached:] = lax.dot_general(
+                grouped(source, r), keys[r], nt, preferred_element_type=F32
+            )
+
+        for r in range(rollouts):
+            score_cached(0, qkv, r)
+
         @pl.when(s > 0)
         def _():
             spread_on(s - 1)
@@ -468,69 +524,70 @@
         new_key = jnp.where(yh == 0, own_kv, other_kv).astype(BF16)
         new_val = jnp.where(yh == 0, other_kv, own_kv).astype(BF16)
         place = pl.ds(pl.multiple_of(s * tokens, tokens), tokens)
-        heads = n_query // HD
-        per = 2 * heads * tokens
-        nt = (((1,), (1,)), ((), ()))
         for r in range(rollouts):
             rows = slice(r * tokens, (r + 1) * tokens)
             keys[r, place, :] = new_key[rows]
             vals[r, place, :] = new_val[rows]
-            parts = [qkv[s, rows, h * HD : (h + 1) * HD] for h in range(heads)]
-            parts += [qkv_in[s, rows, h * HD : (h + 1) * HD] for h in range(heads)]
-            grouped = jnp.concatenate(parts, axis=0)
-            band = slice(r * per, (r + 1) * per)
-            scores[band, :cached] = lax.dot_general(
-                grouped, cache_ref[r, 0, :, :HD], nt, preferred_element_type=F32
-            )
-            scores[band, cached:] = lax.dot_general(grouped, keys[r], nt, preferred_element_type=F32)
-        fresh = scores[:, cached:]
-        key_pos = lax.broadcasted_iota(jnp.int32, fresh.shape, 1)
-        query_pos = lax.rem(lax.broadcasted_iota(jnp.int32, fresh.shape, 0), tokens)
-        allowed = (key_pos <= s * tokens + query_pos) & (yh == 0)
-        fresh = jnp.where(allowed, fresh, -jnp.inf)
-        old = scores[:, :cached]
-        top = jnp.maximum(jnp.max(old, axis=1, keepdims=True), jnp.max(fresh, axis=1, keepdims=True))
-        old = jnp.exp(old - top)
-        fresh = jnp.exp(fresh - top)
-        total = jnp.sum(old, axis=1, keepdims=True) + jnp.sum(fresh, axis=1, keepdims=True)
-        weights[:, :cached] = old.astype(BF16)
-        weights[:, cached:] = fresh.astype(BF16)
-        inverse = 1.0 / total
+            score_cached(1, qkv_in, r)
+            score_new(1, qkv_in, r)
+            score_new(0, qkv, r)
+
+        def soften(group):
+            fresh = scores[group, :, cached:]
+            key_pos = lax.broadcasted_iota(jnp.int32, fresh.shape, 1)
+            query_pos = lax.rem(lax.broadcasted_iota(jnp.int32, fresh.shape, 0), tokens)
+            allowed = (key_pos <= s * tokens + query_pos) & (yh == 0)
+            fresh = jnp.where(allowed, fresh, -jnp.inf)
+            old = scores[group, :, :cached]
+            top = jnp.maximum(jnp.max(old, axis=1, keepdims=True), jnp.max(fresh, axis=1, keepdims=True))
+            old = jnp.exp(old - top)
+            fresh = jnp.exp(fresh - top)
+            total = jnp.sum(old, axis=1, keepdims=True) + jnp.sum(fresh, axis=1, keepdims=True)
+            weights[group, :, :cached] = old.astype(BF16)
+            weights[group, :, cached:] = fresh.astype(BF16)
+            return top, total, 1.0 / total
+
+        def attend(group, r, inverse):
+            summed = jnp.dot(weights[group, band(r), :cached], cache_ref[r, 0, :, HD:], preferred_element_type=F32)
+            summed = summed + jnp.dot(weights[group, band(r), cached:], vals[r], preferred_element_type=F32)
+            return summed * inverse[band(r)]
+
+        far_top, far_total, inverse = soften(1)
         lane = lax.broadcasted_iota(jnp.int32, (tokens, HD), 1)
         for r in range(rollouts):
             rows = slice(r * tokens, (r + 1) * tokens)
-            band = slice(r * per, (r + 1) * per)
-            summed = jnp.dot(weights[band, :cached], cache_ref[r, 0, :, HD:], preferred_element_type=F32)
-            summed = summed + jnp.dot(weights[band, cached:], vals[r], preferred_element_type=F32)
-            summed = summed * inverse[band]
+            summed = attend(1, r, inverse)
             stats = jnp.zeros((tokens, HD), F32)
             for h in range(heads):
-                own_o[rows, h * HD : (h + 1) * HD] = summed[h * tokens : (h + 1) * tokens]
-                far = slice((heads + h) * tokens, (heads + h + 1) * tokens)
-                out_o[s, rows, h * HD : (h + 1) * HD] = summed[far].astype(BF16)
-                left = top[band][far]
-                for piece in range(3):
-                    term = left.astype(BF16).astype(F32)
-                    left = left - term
-                    stats = jnp.where(lane == 8 * h + piece, term, stats)
-                left = total[band][far]
-                for piece in range(3):
-                    term = left.astype(BF16).astype(F32)
-                    left = left - term
-                    stats = jnp.where(lane == 8 * h + 3 + piece, term, stats)
+                at = slice(h * tokens, (h + 1) * tokens)
+                out_o[s, rows, h * HD : (h + 1) * HD] = summed[at].astype(BF16)
+                for first, column in ((8 * h, far_top), (8 * h + 3, far_total)):
+                    left = column[band(r)][at]
+                    for piece in range(3):
+                        term = left.astype(BF16).astype(F32)
+                        left = left - term
+                        stats = jnp.where(lane == first + piece, term, stats)
             out_o[s, rows, n_query:] = stats.astype(BF16)
         swap = copy(out_o.at[s], in_o.at[s], o_send.at[s], o_recv.at[s], pair)
         swap.start()
 
+        top, total, inverse = soften(0)
+        for r in range(rollouts):
+            rows = slice(r * tokens, (r + 1) * tokens)
+            summed = attend(0, r, inverse)
+            for h in range(heads):
+                own_o[rows, h * HD : (h + 1) * HD] = summed[h * tokens : (h + 1) * tokens]
+
         @pl.when(s > 0)
         def _():
             inner_start(s - 1)
 
+        embed_actions(s + 1)
         swap.wait()
 
         stats = in_o[s, :, n_query:].astype(F32)
-        top4 = top.reshape(rollouts, 2 * heads, tokens, 1)
-        total4 = total.reshape(rollouts, 2 * heads, tokens, 1)
+        top4 = top.reshape(rollouts, heads, tokens, 1)
+        total4 = total.reshape(rollouts, heads, tokens, 1)
         joined = []
         for h in range(heads):
             pick = [stats[:, 8 * h + i : 8 * h + i + 1] for i in range(6)]
@@ -559,12 +616,17 @@
             else:
                 terms_q[:, :, j * tile - cut : (j + 1) * tile - cut] = part
 
-        def meanwhile():
+        def hidden_hook():
             @pl.when(s > 0)
             def _():
                 hidden_start(s - 1)
 
-        reduced, sent = scatter(s, meanwhile)
+        def heads_hook():
+            @pl.when(s > 0)
+            def _():
+                heads_start(s - 1)
+
+        reduced, sent = scatter(s, [hidden_hook, heads_hook])
         updated = (state[...] + reduced).astype(BF16).astype(F32)
         state[...] = updated
 
@@ -575,13 +637,9 @@
         spread_start(s)
         for moved in sent:
             moved.wait_send()
-
-        @pl.when(s > 0)
-        def _():
-            heads_start(s - 1)
-
         return carry
 
+    embed_actions(0)
     lax.fori_loop(0, STEPS, step, 0)
     latents_ref[...] = state[...].astype(BF16)
     final = STEPS - 1
@@ -595,7 +653,7 @@
     mine = mine.astype(F32)
     lane = lax.broadcasted_iota(jnp.int32, (rollouts, STEPS), 1)
     all_values = jnp.zeros((rollouts, STEPS), F32)
-    n_actions = head_ref.shape[1]
+    n_actions = head_ref.shape[0]
     for q in range(STEPS):
         policy_end(q)
         now = jnp.dot(
@@ -630,7 +688,7 @@
     n_query = w_query.shape[1]
     wide = n_query + w_keyval.shape[1]
     cached = cache.shape[2]
-    bands = n_rows * 2 * (n_query // HD)
+    bands = n_rows * (n_query // HD)
     units = policy_mid.shape[2] // n_tensor
     cut = PAIR_COLUMNS
     vmem = pl.BlockSpec(memory_space=pltpu.VMEM)
@@ -642,9 +700,14 @@
             jax.ShapeDtypeStruct((rollouts, STEPS, policy_head.shape[2]), F32),
             jax.ShapeDtypeStruct((rollouts, STEPS), F32),
         ),
-        in_specs=[vmem] * 13,
+        in_specs=[vmem] * 5 + [pl.BlockSpec(memory_space=pl.ANY)] * 6 + [vmem] * 2,
         out_specs=(vmem,) * 3,
         scratch_shapes=[
+            pltpu.VMEM(big.shape, BF16)
+            for big in (cache, w_query, w_keyval, w_out, policy_in, policy_mid)
+        ]
+        + [
+            pltpu.VMEM((rollouts, width), F32),
             pltpu.VMEM((rollouts, width), F32),
             pltpu.VMEM((STEPS, n_tensor, 16, cut), BF16),
             pltpu.VMEM((STEPS, n_tensor, 16, half - cut), BF16),
@@ -652,8 +715,8 @@
             pltpu.VMEM((STEPS, n_rows, wide), BF16),
             pltpu.VMEM((rollouts, 128, HD), BF16),
             pltpu.VMEM((rollouts, 128, HD), BF16),
-            pltpu.VMEM((bands, cached + 128), F32),
-            pltpu.VMEM((bands, cached + 128), BF16),
+            pltpu.VMEM((2, bands, cached + 128), F32),
+            pltpu.VMEM((2, bands, cached + 128), BF16),
             pltpu.VMEM((n_rows, n_query), F32),
             pltpu.VMEM((STEPS, n_rows, wide), BF16),
             pltpu.VMEM((STEPS, n_rows, wide), BF16),
@@ -680,15 +743,16 @@
         + [dma((STEPS, n_z)), dma((STEPS, 2))]
         + [dma((STEPS, peers))] * 2
         + [dma((STEPS, n_tensor))] * 4
-        + [dma((STEPS, peers))] * 2,
+        + [dma((STEPS, peers))] * 2
+        + [dma((6,))],
         compiler_params=pltpu.CompilerParams(
             collective_id=0, has_side_effects=True, vmem_limit_bytes=VMEM_LIMIT
         ),
         name="imagine",
     )(
         frame.reshape(rollouts, width),
-        actions,
-        owners,
+        actions.T,
+        owners.T,
         attn_gain.reshape(1, width),
         action_table,
         cache,
@@ -697,7 +761,7 @@
         w_out,
         policy_in,
         policy_mid,
-        policy_head.reshape(policy_head.shape[1:]),
+        policy_head.reshape(policy_head.shape[1:]).T,
         policy_value,
     )
     return (latents.reshape(frame.shape), log_probs, values)

time: 277 us -> 276 us (level)
  local copies, waits for them, and re-layouts: 8.77 us -> 4.18 us
  Pallas kernels: 267 us -> 271 us
    unnamed x6 -> x3, local copies, waits for them, and re-layouts: 8.77 us -> 4.18 us
    pallas_call x1, Pallas kernels: 267 us -> 271 us  [shards(): pl.pallas_call(functools.partial(kernel, n_z, peers), out_shape=(jax.Shap...]
where the time goes in v3:
time: 276 us
  Pallas kernels  271 us (98%)
  local copies, waits for them, and re-layouts  4.18 us (2%)
    pallas_call x1, Pallas kernels, shards(): pl.pallas_call(functools.partial(kernel, n_z, peers), out_shape=(jax.Shap...  271 us

profile of v3, /device:TPU:8, one launch (start us, length us, event | category | flops | bytes accessed | tf_op | source)
XLA Modules:
  0.0 276.0 jit_solution(5130310731155204569)
XLA Ops:
  0.6 271.2 %imagine.1 = (bf16[8,5120]{1,0:T(8,128)(2,1)}, f32[8,4,18]{2,1,0:T(4,128)}, f32[8,4]{1,0:T(8,128)}) custom-call(bf16[8,5120]{1,0:T(8,128)(2,1)} %bitcast.9, s32[4,8]{1,0:T(4,128)} %bitcast.12, s32[1,8]{1,0:T(1,128)} %bitcast.13, f32[1,5120]{1,0:T(1,128)} %bitcast.11, bf16[18,5120]{1,0:T(8,128)(2,1)} %table_ref.1, bf16[8,1,512,256]{3,2,1,0:T(8,128)(2,1)} %cache_hbm.1, ...), custom_call_target="tpu_custom_call" | custom-call | tf_op jit(solution)/shard_map/imagine/pallas_call | solution.py:696
  271.9 1.3 copy.16
  273.2 1.5 copy.19
  274.7 1.3 copy.20

commit v4 on v3

--- a/solution.py
+++ b/solution.py
@@ -1,4 +1,5 @@
 import functools
+import typing
 
 import jax
 import jax.numpy as jnp
@@ -28,6 +29,28 @@
 
 PAIR_COLUMNS = 512
 FAR = {False: {1: 0, -1: 0, 2: 0, -2: 0, 3: 2, -3: -2, 4: 2}, True: {1: 0, -1: 0, 2: 0, -2: 0, 3: 2, -3: -2, -4: -2}}
+
+
+BATCHES = ((0, 1, 2), (3,))
+
+
+class Batch(typing.NamedTuple):
+    steps: tuple
+    outgoing: typing.Any
+    arrived: typing.Any
+    partial: typing.Any
+    partial_in: typing.Any
+    hidden: typing.Any
+    answers: typing.Any
+    returned: typing.Any
+    a_send: typing.Any
+    a_recv: typing.Any
+    h_send: typing.Any
+    h_recv: typing.Any
+    g_send: typing.Any
+    g_recv: typing.Any
+    b_send: typing.Any
+    b_recv: typing.Any
 
 
 def due(tree, k):
@@ -102,13 +125,6 @@
     pair_p,
     pair_q,
     latent_rows,
-    outgoing,
-    arrived,
-    partial,
-    partial_in,
-    hidden,
-    answers,
-    returned,
     ag_zs,
     ag_zr,
     ag_ys,
@@ -123,16 +139,10 @@
     o_recv,
     l_send,
     l_recv,
-    a_send,
-    a_recv,
-    h_send,
-    h_recv,
-    g_send,
-    g_recv,
-    b_send,
-    b_recv,
     loaded,
+    *batch_refs,
 ):
+    batches = [Batch(steps, *batch_refs[i * 15 : (i + 1) * 15]) for i, steps in enumerate(BATCHES)]
     loads = [
         pltpu.make_async_copy(src, dst, loaded.at[i])
         for i, (src, dst) in enumerate(
@@ -215,49 +225,48 @@
     nt = (((1,), (1,)), ((), ()))
     pl.semaphore_wait(barrier, peers + n_tensor - 2)
 
-    def spread_out(q, k):
+    def spread_across(q, k):
         mine = latent_rows.at[q]
-        for c in below(FAR[False], k):
-            copy(mine, mine, l_send.at[q, c % n_z], l_recv.at[q, 0], to_plane(c - k)).start()
-        copy(mine, mine, l_send.at[q, 0], l_recv.at[q, 1], pair).start()
-
-    def spread_sent(q, k):
+        return copy(mine, mine, l_send.at[q, k], l_recv.at[q, 0], to_plane(k))
+
+    def spread_pair(q):
         mine = latent_rows.at[q]
-        for c in below(FAR[False], k):
-            copy(mine, mine, l_send.at[q, c % n_z], l_recv.at[q, 0], to_plane(c - k)).wait_send()
-        copy(mine, mine, l_send.at[q, 0], l_recv.at[q, 1], pair).wait_send()
+        return copy(mine, mine, l_send.at[q, 0], l_recv.at[q, 1], pair)
+
+    far_first = sorted(range(1, n_z), key=lambda k: -min(k, n_z - k))
 
     def spread_start(q):
         @pl.when(tensor == last)
         def _():
-            spread_out(q, 0)
+            for k in far_first:
+                spread_across(q, k).start()
+            spread_pair(q).start()
 
     def spread_on(q):
-        mine = latent_rows.at[q]
-        for k in FAR[False]:
-
-            @pl.when(tensor == (last + 2 * k) % n_tensor)
-            def _():
-                copy(mine, mine, l_send.at[q, 0], l_recv.at[q, 0], pair).wait_recv()
-                spread_out(q, k)
-
+        @pl.when((yh == 1) & (tensor != last))
+        def _():
+            spread_across(q, 1).wait_recv()
+            spread_pair(q).start()
+
+    def spread_end(q):
         @pl.when(yh == 0)
         def _():
-            copy(mine, mine, l_send.at[q, 0], l_recv.at[q, 1], pair).wait_recv()
-
-    def spread_end(q):
-        for k in [0] + list(FAR[False]):
-
-            @pl.when(tensor == (last + 2 * k) % n_tensor)
-            def _():
-                spread_sent(q, k)
-
-    def route(q, k):
-        return copy(
-            outgoing.at[q, lax.rem(row + k, peers)], arrived.at[q, row], a_send.at[q, k], a_recv.at[q, k], to_row(k)
-        )
-
-    def route_start(q):
+            spread_pair(q).wait_recv()
+
+    def spread_sent(q):
+        @pl.when(yh == 1)
+        def _():
+            spread_pair(q).wait_send()
+
+        @pl.when(tensor == last)
+        def _():
+            for k in far_first:
+                spread_across(q, k).wait_send()
+
+    def route(b, k):
+        return copy(b.outgoing.at[lax.rem(row + k, peers)], b.arrived.at[row], b.a_send.at[k], b.a_recv.at[k], to_row(k))
+
+    def route_start(b):
         wide = half // 4
         i = lax.broadcasted_iota(jnp.int32, (16, spots), 1)
         j = lax.broadcasted_iota(jnp.int32, (16, spots), 0)
@@ -265,92 +274,97 @@
         place2 = jnp.concatenate([place_of, place_of], axis=0)
         chosen = (i // 16 == owner2) & (lax.rem(i, CAP).astype(F32) == place2)
         eighth = lax.rem(i // CAP, eighths)
-        built = jnp.zeros((spots, wide), F32)
-        for quarter in range(4):
-            hot = (chosen & (eighth == (j // rollouts) * 4 + quarter)).astype(F32).astype(BF16)
-            built = built + lax.dot_general(
-                hot, latent_rows[q, :, quarter * wide : (quarter + 1) * wide], tn, preferred_element_type=F32
-            )
-        outgoing[q] = built.astype(BF16).reshape(peers, 16, wide)
-        arrived[q, row] = outgoing[q, row]
+        hots = [
+            (chosen & (eighth == (j // rollouts) * 4 + quarter)).astype(F32).astype(BF16) for quarter in range(4)
+        ]
+        for n, q in enumerate(b.steps):
+            built = jnp.zeros((spots, wide), F32)
+            for quarter in range(4):
+                built = built + lax.dot_general(
+                    hots[quarter],
+                    latent_rows[q, :, quarter * wide : (quarter + 1) * wide],
+                    tn,
+                    preferred_element_type=F32,
+                )
+            b.outgoing[:, n * 16 : (n + 1) * 16, :] = built.astype(BF16).reshape(peers, 16, wide)
         for k in range(1, peers):
-            route(q, k).start()
-
-    def to_units(q, k):
+            route(b, k).start()
+        b.arrived[row] = b.outgoing[row]
+
+    def to_units(b, k):
         return copy(
-            partial.at[q, lax.rem(tensor + k, n_tensor)],
-            partial_in.at[q, k],
-            h_send.at[q, k],
-            h_recv.at[q, k],
-            to_tensor(k),
+            b.partial.at[lax.rem(tensor + k, n_tensor)], b.partial_in.at[k], b.h_send.at[k], b.h_recv.at[k], to_tensor(k)
         )
 
-    def inner_start(q):
+    def inner_start(b):
         for k in range(1, peers):
-            origin = arrived.at[q, lax.rem(row + peers - k, peers)]
-            copy(origin, origin, a_send.at[q, k], a_recv.at[q, k], to_row(k)).wait_recv()
+            origin = b.arrived.at[lax.rem(row + peers - k, peers)]
+            copy(origin, origin, b.a_send.at[k], b.a_recv.at[k], to_row(k)).wait_recv()
         wide = half // 4
-        rows = arrived[q].reshape(spots, wide)
+        tall = len(b.steps) * 16
+        rows = b.arrived[...].reshape(peers * tall, wide)
         n_inner = pin_ref.shape[2]
-        at_row = lax.rem(lax.broadcasted_iota(jnp.int32, (spots, n_inner), 0) // CAP, eighths)
-        picked = jnp.zeros((spots, n_inner), F32)
+        at_row = lax.rem(lax.broadcasted_iota(jnp.int32, (peers * tall, n_inner), 0) // CAP, eighths)
+        picked = jnp.zeros((peers * tall, n_inner), F32)
         for e in range(eighths):
             product = jnp.dot(rows, pin_ref[0, e * wide : (e + 1) * wide, :], preferred_element_type=F32)
             picked = picked + jnp.where(at_row == e, product, 0.0)
-        i = lax.broadcasted_iota(jnp.int32, (16, spots), 1)
-        j = lax.broadcasted_iota(jnp.int32, (16, spots), 0)
-        gather = ((i // 16 == j // CAP) & (lax.rem(i, CAP) == lax.rem(j, CAP))).astype(F32)
-        before_silu = jnp.dot(gather, picked, preferred_element_type=F32, precision=lax.Precision.HIGHEST)
+        i = lax.broadcasted_iota(jnp.int32, (tall, peers * tall), 1)
+        j = lax.broadcasted_iota(jnp.int32, (tall, peers * tall), 0)
+        collect = (i // tall == lax.rem(j, 16) // CAP) & (lax.rem(i, tall) // 16 == j // 16)
+        collect = (collect & (lax.rem(i, CAP) == lax.rem(j, CAP))).astype(F32)
+        before_silu = jnp.dot(collect, picked, preferred_element_type=F32, precision=lax.Precision.HIGHEST)
         inner = silu(before_silu).astype(BF16)
-        units = partial.shape[3]
+        units = b.partial.shape[2]
         product = jnp.dot(inner, pmid_ref[0], preferred_element_type=F32).astype(BF16)
         for t in range(n_tensor):
-            partial[q, t] = product[:, t * units : (t + 1) * units]
+            b.partial[t] = product[:, t * units : (t + 1) * units]
         for k in range(1, n_tensor):
-            to_units(q, k).start()
-
-    def share(q, k):
-        mine = hidden.at[q, tensor]
-        return copy(mine, mine, g_send.at[q, k], g_recv.at[q, k], to_tensor(k))
-
-    def hidden_start(q):
-        summed = partial[q, tensor].astype(F32)
+            to_units(b, k).start()
+
+    def share(b, k):
+        mine = b.hidden.at[tensor]
+        return copy(mine, mine, b.g_send.at[k], b.g_recv.at[k], to_tensor(k))
+
+    def hidden_start(b):
+        summed = b.partial[tensor].astype(F32)
         for k in range(1, n_tensor):
-            to_units(q, k).wait_recv()
-            summed = summed + partial_in[q, k].astype(F32)
-        hidden[q, tensor] = silu(summed).astype(BF16)
+            to_units(b, k).wait_recv()
+            summed = summed + b.partial_in[k].astype(F32)
+        b.hidden[tensor] = silu(summed).astype(BF16)
         for k in range(1, n_tensor):
-            share(q, k).start()
-
-    def reply(q, k):
-        return copy(answers.at[q], returned.at[q, row], b_send.at[q, k], b_recv.at[q, k], to_row(k))
-
-    def heads_start(q):
+            share(b, k).start()
+
+    def reply(b, k):
+        return copy(b.answers, b.returned.at[row], b.b_send.at[k], b.b_recv.at[k], to_row(k))
+
+    def heads_start(b):
         for k in range(1, n_tensor):
-            origin = hidden.at[q, lax.rem(tensor + n_tensor - k, n_tensor)]
-            copy(origin, origin, g_send.at[q, k], g_recv.at[q, k], to_tensor(k)).wait_recv()
-        whole = jnp.concatenate([hidden[q, t] for t in range(n_tensor)], axis=1)
+            origin = b.hidden.at[lax.rem(tensor + n_tensor - k, n_tensor)]
+            copy(origin, origin, b.g_send.at[k], b.g_recv.at[k], to_tensor(k)).wait_recv()
+        whole = jnp.concatenate([b.hidden[t] for t in range(n_tensor)], axis=1)
         logits = lax.dot_general(whole, head_ref[...], nt, preferred_element_type=F32)
         value = jnp.sum(whole.astype(F32) * critic_ref[...].astype(F32), axis=1, keepdims=True)
         peak = jnp.max(logits, axis=1, keepdims=True)
         logp = logits - (peak + jnp.log(jnp.sum(jnp.exp(logits - peak), axis=1, keepdims=True)))
-        blank = jnp.zeros((16, 128 - logits.shape[1] - 1), F32)
-        answers[q] = jnp.concatenate([logp, value, blank], axis=1)
-        returned[q, row] = answers[q]
+        blank = jnp.zeros((logits.shape[0], 128 - logits.shape[1] - 1), F32)
+        b.answers[...] = jnp.concatenate([logp, value, blank], axis=1)
         for k in range(1, peers):
-            reply(q, k).start()
-
-    def policy_end(q):
+            reply(b, k).start()
+        b.returned[row] = b.answers[...]
+
+    def replies_wait(b):
         for k in range(1, peers):
-            origin = returned.at[q, lax.rem(row + peers - k, peers)]
-            copy(origin, origin, b_send.at[q, k], b_recv.at[q, k], to_row(k)).wait_recv()
-        spread_end(q)
+            origin = b.returned.at[lax.rem(row + peers - k, peers)]
+            copy(origin, origin, b.b_send.at[k], b.b_recv.at[k], to_row(k)).wait_recv()
+
+    def batch_sent(b):
         for k in range(1, peers):
-            route(q, k).wait_send()
-            reply(q, k).wait_send()
+            route(b, k).wait_send()
+            reply(b, k).wait_send()
         for k in range(1, n_tensor):
-            to_units(q, k).wait_send()
-            share(q, k).wait_send()
+            to_units(b, k).wait_send()
+            share(b, k).wait_send()
 
     def gather(s):
         own, other, front = FAR[False], FAR[True], FAR[False]
@@ -414,7 +428,7 @@
             events += [(offset + deepest - due(trees[stream], k), stream, k) for k in [0] + list(trees[stream])]
         ends = {}
         for number, (_, stream, k) in enumerate(sorted(events)):
-            if number in (len(events) // 2, len(events) * 7 // 8):
+            if number in (0, len(events) // 2):
                 hooks.pop(0)()
             tree = trees[stream]
             terms = terms_q if stream == 2 else terms_p
@@ -512,8 +526,7 @@
 
         @pl.when(s > 0)
         def _():
-            spread_on(s - 1)
-            route_start(s - 1)
+            spread_start(s - 1)
 
         for moved in gathered:
             moved.wait_send()
@@ -578,10 +591,6 @@
             for h in range(heads):
                 own_o[rows, h * HD : (h + 1) * HD] = summed[h * tokens : (h + 1) * tokens]
 
-        @pl.when(s > 0)
-        def _():
-            inner_start(s - 1)
-
         embed_actions(s + 1)
         swap.wait()
 
@@ -616,17 +625,21 @@
             else:
                 terms_q[:, :, j * tile - cut : (j + 1) * tile - cut] = part
 
-        def hidden_hook():
+        def spread_hook():
             @pl.when(s > 0)
             def _():
-                hidden_start(s - 1)
-
-        def heads_hook():
+                spread_on(s - 1)
+
+        def route_hook():
             @pl.when(s > 0)
             def _():
-                heads_start(s - 1)
-
-        reduced, sent = scatter(s, [hidden_hook, heads_hook])
+                spread_end(s - 1)
+
+            @pl.when(s == STEPS - 1)
+            def _():
+                route_start(batches[0])
+
+        reduced, sent = scatter(s, [spread_hook, route_hook])
         updated = (state[...] + reduced).astype(BF16).astype(F32)
         state[...] = updated
 
@@ -634,30 +647,42 @@
         def _():
             latent_rows[s] = folded(rms_rows(updated)).astype(BF16)
 
-        spread_start(s)
         for moved in sent:
             moved.wait_send()
         return carry
 
     embed_actions(0)
     lax.fori_loop(0, STEPS, step, 0)
+    final = STEPS - 1
+    spread_start(final)
+    inner_start(batches[0])
+    spread_on(final)
+    hidden_start(batches[0])
+    spread_end(final)
+    route_start(batches[1])
+    heads_start(batches[0])
     latents_ref[...] = state[...].astype(BF16)
-    final = STEPS - 1
-    spread_on(final)
-    route_start(final)
-    inner_start(final)
-    hidden_start(final)
-    heads_start(final)
+    inner_start(batches[1])
+    for q in range(STEPS):
+        spread_sent(q)
+    hidden_start(batches[1])
+    replies_wait(batches[0])
+    heads_start(batches[1])
+    for b in batches:
+        batch_sent(b)
+    replies_wait(batches[1])
     i = lax.broadcasted_iota(jnp.int32, (rollouts, spots), 1)
     mine = (i // 16 == owner) & (lax.rem(i, CAP).astype(F32) == place_of) & (lax.rem(i // CAP, eighths) == row)
     mine = mine.astype(F32)
     lane = lax.broadcasted_iota(jnp.int32, (rollouts, STEPS), 1)
     all_values = jnp.zeros((rollouts, STEPS), F32)
     n_actions = head_ref.shape[0]
-    for q in range(STEPS):
-        policy_end(q)
+    for q, b, n in [(q, b, n) for b in batches for n, q in enumerate(b.steps)]:
         now = jnp.dot(
-            mine, returned[q].reshape(spots, 128), preferred_element_type=F32, precision=lax.Precision.HIGHEST
+            mine,
+            b.returned[:, n * 16 : (n + 1) * 16, :].reshape(spots, 128),
+            preferred_element_type=F32,
+            precision=lax.Precision.HIGHEST,
         )
         logp_ref[:, q, :] = now[:, :n_actions]
         all_values = jnp.where(lane == q, now[:, n_actions : n_actions + 1], all_values)
@@ -693,6 +718,18 @@
     cut = PAIR_COLUMNS
     vmem = pl.BlockSpec(memory_space=pltpu.VMEM)
     dma = pltpu.SemaphoreType.DMA
+
+    def batch_scratch(count):
+        tall = count * 16
+        return (
+            [pltpu.VMEM((peers, tall, half // 4), BF16)] * 2
+            + [pltpu.VMEM((n_tensor, tall, units), BF16)] * 3
+            + [pltpu.VMEM((tall, 128), F32), pltpu.VMEM((peers, tall, 128), F32)]
+            + [dma((peers,))] * 2
+            + [dma((n_tensor,))] * 4
+            + [dma((peers,))] * 2
+        )
+
     latents, log_probs, values = pl.pallas_call(
         functools.partial(kernel, n_z, peers),
         out_shape=(
@@ -727,13 +764,6 @@
             pltpu.VMEM((STEPS, 16, cut), BF16),
             pltpu.VMEM((STEPS, n_z, 16, half - cut), BF16),
             pltpu.VMEM((STEPS, 16, half), BF16),
-            pltpu.VMEM((STEPS, peers, 16, half // 4), BF16),
-            pltpu.VMEM((STEPS, peers, 16, half // 4), BF16),
-            pltpu.VMEM((STEPS, n_tensor, 16, units), BF16),
-            pltpu.VMEM((STEPS, n_tensor, 16, units), BF16),
-            pltpu.VMEM((STEPS, n_tensor, 16, units), BF16),
-            pltpu.VMEM((STEPS, 16, 128), F32),
-            pltpu.VMEM((STEPS, peers, 16, 128), F32),
         ]
         + [dma((STEPS, 3, n_z))] * 2
         + [dma((STEPS, n_z + 1))] * 2
@@ -741,10 +771,8 @@
         + [dma((STEPS, n_z + 1))] * 2
         + [dma((STEPS,))] * 4
         + [dma((STEPS, n_z)), dma((STEPS, 2))]
-        + [dma((STEPS, peers))] * 2
-        + [dma((STEPS, n_tensor))] * 4
-        + [dma((STEPS, peers))] * 2
-        + [dma((6,))],
+        + [dma((6,))]
+        + [ref for steps in BATCHES for ref in batch_scratch(len(steps))],
         compiler_params=pltpu.CompilerParams(
             collective_id=0, has_side_effects=True, vmem_limit_bytes=VMEM_LIMIT
         ),

time: 276 us -> 263 us (0.953)
  Pallas kernels: 271 us -> 258 us
    pallas_call x1, Pallas kernels: 271 us -> 258 us  [shards(): pl.pallas_call(functools.partial(kernel, n_z, peers), out_shape=(jax.Shap...]
where the time goes in v4:
time: 263 us
  Pallas kernels  258 us (98%)
  local copies, waits for them, and re-layouts  4.18 us (2%)
    pallas_call x1, Pallas kernels, shards(): pl.pallas_call(functools.partial(kernel, n_z, peers), out_shape=(jax.Shap...  258 us

profile of v4, /device:TPU:8, one launch (start us, length us, event | category | flops | bytes accessed | tf_op | source)
XLA Modules:
  0.0 262.6 jit_solution(3160984862800713772)
XLA Ops:
  0.6 257.7 %imagine.1 = (bf16[8,5120]{1,0:T(8,128)(2,1)}, f32[8,4,18]{2,1,0:T(4,128)}, f32[8,4]{1,0:T(8,128)}) custom-call(bf16[8,5120]{1,0:T(8,128)(2,1)} %bitcast.9, s32[4,8]{1,0:T(4,128)} %bitcast.12, s32[1,8]{1,0:T(1,128)} %bitcast.13, f32[1,5120]{1,0:T(1,128)} %bitcast.11, bf16[18,5120]{1,0:T(8,128)(2,1)} %table_ref.1, bf16[8,1,512,256]{3,2,1,0:T(8,128)(2,1)} %cache_hbm.1, ...), custom_call_target="tpu_custom_call" | custom-call | tf_op jit(solution)/shard_map/imagine/pallas_call | solution.py:733
  258.4 1.3 copy.16
  259.7 1.5 copy.19
  261.2 1.3 copy.20

commit v5 on v4

--- a/solution.py
+++ b/solution.py
@@ -28,6 +28,7 @@
 
 
 PAIR_COLUMNS = 512
+PARTS = 2
 FAR = {False: {1: 0, -1: 0, 2: 0, -2: 0, 3: 2, -3: -2, 4: 2}, True: {1: 0, -1: 0, 2: 0, -2: 0, 3: 2, -3: -2, -4: -2}}
 
 
@@ -498,8 +499,17 @@
         n_query = query.shape[1]
         qkv[s, :, :n_query] = jnp.dot(by_rollout, query, preferred_element_type=F32).astype(BF16)
         qkv[s, :, n_query:] = jnp.dot(by_rollout, keyval, preferred_element_type=F32).astype(BF16)
-        swap = copy(qkv.at[s], qkv_in.at[s], q_send.at[s], q_recv.at[s], pair)
-        swap.start()
+        part_rows = n_rows // PARTS
+
+        def parted(n):
+            return pl.ds(n * part_rows, part_rows)
+
+        swaps = [
+            copy(qkv.at[s, parted(n)], qkv_in.at[s, parted(n)], q_send.at[s, n], q_recv.at[s, n], pair)
+            for n in range(PARTS)
+        ]
+        for swap in swaps:
+            swap.start()
 
         heads = n_query // HD
         per = heads * tokens
@@ -530,69 +540,80 @@
 
         for moved in gathered:
             moved.wait_send()
-        swap.wait()
-
-        own_kv = qkv[s, :, n_query:].astype(F32)
-        other_kv = qkv_in[s, :, n_query:].astype(F32)
-        new_key = jnp.where(yh == 0, own_kv, other_kv).astype(BF16)
-        new_val = jnp.where(yh == 0, other_kv, own_kv).astype(BF16)
         place = pl.ds(pl.multiple_of(s * tokens, tokens), tokens)
-        for r in range(rollouts):
-            rows = slice(r * tokens, (r + 1) * tokens)
-            keys[r, place, :] = new_key[rows]
-            vals[r, place, :] = new_val[rows]
-            score_cached(1, qkv_in, r)
-            score_new(1, qkv_in, r)
-            score_new(0, qkv, r)
-
-        def soften(group):
-            fresh = scores[group, :, cached:]
+
+        def soften(group, low, high):
+            fresh = scores[group, low:high, cached:]
             key_pos = lax.broadcasted_iota(jnp.int32, fresh.shape, 1)
             query_pos = lax.rem(lax.broadcasted_iota(jnp.int32, fresh.shape, 0), tokens)
             allowed = (key_pos <= s * tokens + query_pos) & (yh == 0)
             fresh = jnp.where(allowed, fresh, -jnp.inf)
-            old = scores[group, :, :cached]
+            old = scores[group, low:high, :cached]
             top = jnp.maximum(jnp.max(old, axis=1, keepdims=True), jnp.max(fresh, axis=1, keepdims=True))
             old = jnp.exp(old - top)
             fresh = jnp.exp(fresh - top)
             total = jnp.sum(old, axis=1, keepdims=True) + jnp.sum(fresh, axis=1, keepdims=True)
-            weights[group, :, :cached] = old.astype(BF16)
-            weights[group, :, cached:] = fresh.astype(BF16)
+            weights[group, low:high, :cached] = old.astype(BF16)
+            weights[group, low:high, cached:] = fresh.astype(BF16)
             return top, total, 1.0 / total
 
         def attend(group, r, inverse):
             summed = jnp.dot(weights[group, band(r), :cached], cache_ref[r, 0, :, HD:], preferred_element_type=F32)
             summed = summed + jnp.dot(weights[group, band(r), cached:], vals[r], preferred_element_type=F32)
-            return summed * inverse[band(r)]
-
-        far_top, far_total, inverse = soften(1)
+            return summed * inverse
+
         lane = lax.broadcasted_iota(jnp.int32, (tokens, HD), 1)
+        sums = [
+            copy(out_o.at[s, parted(n)], in_o.at[s, parted(n)], o_send.at[s, n], o_recv.at[s, n], pair)
+            for n in range(PARTS)
+        ]
+        per_part = rollouts // PARTS
+        for n in range(PARTS):
+            swaps[n].wait_recv()
+            here = slice(n * part_rows, (n + 1) * part_rows)
+            own_kv = qkv[s, here, n_query:].astype(F32)
+            other_kv = qkv_in[s, here, n_query:].astype(F32)
+            new_key = jnp.where(yh == 0, own_kv, other_kv).astype(BF16)
+            new_val = jnp.where(yh == 0, other_kv, own_kv).astype(BF16)
+            for i in range(per_part):
+                r = n * per_part + i
+                rows = slice(i * tokens, (i + 1) * tokens)
+                keys[r, place, :] = new_key[rows]
+                vals[r, place, :] = new_val[rows]
+                score_cached(1, qkv_in, r)
+                score_new(1, qkv_in, r)
+            far_top, far_total, inverse = soften(1, n * per_part * per, (n + 1) * per_part * per)
+            for i in range(per_part):
+                r = n * per_part + i
+                rows = slice(r * tokens, (r + 1) * tokens)
+                summed = attend(1, r, inverse[band(i)])
+                stats = jnp.zeros((tokens, HD), F32)
+                for h in range(heads):
+                    at = slice(h * tokens, (h + 1) * tokens)
+                    out_o[s, rows, h * HD : (h + 1) * HD] = summed[at].astype(BF16)
+                    for first, column in ((8 * h, far_top), (8 * h + 3, far_total)):
+                        left = column[band(i)][at]
+                        for piece in range(3):
+                            term = left.astype(BF16).astype(F32)
+                            left = left - term
+                            stats = jnp.where(lane == first + piece, term, stats)
+                out_o[s, rows, n_query:] = stats.astype(BF16)
+            sums[n].start()
+
+        for r in range(rollouts):
+            score_new(0, qkv, r)
+        top, total, inverse = soften(0, 0, rollouts * per)
         for r in range(rollouts):
             rows = slice(r * tokens, (r + 1) * tokens)
-            summed = attend(1, r, inverse)
-            stats = jnp.zeros((tokens, HD), F32)
-            for h in range(heads):
-                at = slice(h * tokens, (h + 1) * tokens)
-                out_o[s, rows, h * HD : (h + 1) * HD] = summed[at].astype(BF16)
-                for first, column in ((8 * h, far_top), (8 * h + 3, far_total)):
-                    left = column[band(r)][at]
-                    for piece in range(3):
-                        term = left.astype(BF16).astype(F32)
-                        left = left - term
-                        stats = jnp.where(lane == first + piece, term, stats)
-            out_o[s, rows, n_query:] = stats.astype(BF16)
-        swap = copy(out_o.at[s], in_o.at[s], o_send.at[s], o_recv.at[s], pair)
-        swap.start()
-
-        top, total, inverse = soften(0)
-        for r in range(rollouts):
-            rows = slice(r * tokens, (r + 1) * tokens)
-            summed = attend(0, r, inverse)
+            summed = attend(0, r, inverse[band(r)])
             for h in range(heads):
                 own_o[rows, h * HD : (h + 1) * HD] = summed[h * tokens : (h + 1) * tokens]
 
         embed_actions(s + 1)
-        swap.wait()
+        for swap in swaps:
+            swap.wait_send()
+        for swap in sums:
+            swap.wait()
 
         stats = in_o[s, :, n_query:].astype(F32)
         top4 = top.reshape(rollouts, heads, tokens, 1)
@@ -769,7 +790,7 @@
         + [dma((STEPS, n_z + 1))] * 2
         + [dma((STEPS, 3, n_z))] * 2
         + [dma((STEPS, n_z + 1))] * 2
-        + [dma((STEPS,))] * 4
+        + [dma((STEPS, PARTS))] * 4
         + [dma((STEPS, n_z)), dma((STEPS, 2))]
         + [dma((6,))]
         + [ref for steps in BATCHES for ref in batch_scratch(len(steps))],

time: 263 us -> 258 us (0.981)
  Pallas kernels: 258 us -> 253 us
    pallas_call x1, Pallas kernels: 258 us -> 253 us  [shards(): pl.pallas_call(functools.partial(kernel, n_z, peers), out_shape=(jax.Shap...]
where the time goes in v5:
time: 258 us
  Pallas kernels  253 us (98%)
  local copies, waits for them, and re-layouts  4.18 us (2%)
    pallas_call x1, Pallas kernels, shards(): pl.pallas_call(functools.partial(kernel, n_z, peers), out_shape=(jax.Shap...  253 us

profile of v5, /device:TPU:8, one launch (start us, length us, event | category | flops | bytes accessed | tf_op | source)
XLA Modules:
  0.0 258.0 jit_solution(651378837149857206)
XLA Ops:
  0.6 253.2 %imagine.1 = (bf16[8,5120]{1,0:T(8,128)(2,1)}, f32[8,4,18]{2,1,0:T(4,128)}, f32[8,4]{1,0:T(8,128)}) custom-call(bf16[8,5120]{1,0:T(8,128)(2,1)} %bitcast.9, s32[4,8]{1,0:T(4,128)} %bitcast.12, s32[1,8]{1,0:T(1,128)} %bitcast.13, f32[1,5120]{1,0:T(1,128)} %bitcast.11, bf16[18,5120]{1,0:T(8,128)(2,1)} %table_ref.1, bf16[8,1,512,256]{3,2,1,0:T(8,128)(2,1)} %cache_hbm.1, ...), custom_call_target="tpu_custom_call" | custom-call | tf_op jit(solution)/shard_map/imagine/pallas_call | solution.py:754
  253.8 1.3 copy.16
  255.1 1.5 copy.19
  256.7 1.3 copy.20

commit v6 on v5

--- a/solution.py
+++ b/solution.py
@@ -226,48 +226,54 @@
     nt = (((1,), (1,)), ((), ()))
     pl.semaphore_wait(barrier, peers + n_tensor - 2)
 
-    def spread_across(q, k):
-        mine = latent_rows.at[q]
-        return copy(mine, mine, l_send.at[q, k], l_recv.at[q, 0], to_plane(k))
-
-    def spread_pair(q):
-        mine = latent_rows.at[q]
-        return copy(mine, mine, l_send.at[q, 0], l_recv.at[q, 1], pair)
+    def spread_across(q, piece, k):
+        mine = latent_rows.at[q, piece]
+        return copy(mine, mine, l_send.at[q, piece, k], l_recv.at[q, piece, 0], to_plane(k))
+
+    def spread_pair(q, piece):
+        mine = latent_rows.at[q, piece]
+        return copy(mine, mine, l_send.at[q, piece, 0], l_recv.at[q, piece, 1], pair)
 
     far_first = sorted(range(1, n_z), key=lambda k: -min(k, n_z - k))
+    pieces = range(latent_rows.shape[1])
 
     def spread_start(q):
         @pl.when(tensor == last)
         def _():
-            for k in far_first:
-                spread_across(q, k).start()
-            spread_pair(q).start()
+            for piece in pieces:
+                for k in far_first:
+                    spread_across(q, piece, k).start()
+                spread_pair(q, piece).start()
 
     def spread_on(q):
         @pl.when((yh == 1) & (tensor != last))
         def _():
-            spread_across(q, 1).wait_recv()
-            spread_pair(q).start()
+            for piece in pieces:
+                spread_across(q, piece, 1).wait_recv()
+                spread_pair(q, piece).start()
 
     def spread_end(q):
         @pl.when(yh == 0)
         def _():
-            spread_pair(q).wait_recv()
+            for piece in pieces:
+                spread_pair(q, piece).wait_recv()
 
     def spread_sent(q):
         @pl.when(yh == 1)
         def _():
-            spread_pair(q).wait_send()
+            for piece in pieces:
+                spread_pair(q, piece).wait_send()
 
         @pl.when(tensor == last)
         def _():
-            for k in far_first:
-                spread_across(q, k).wait_send()
+            for piece in pieces:
+                for k in far_first:
+                    spread_across(q, piece, k).wait_send()
 
     def route(b, k):
         return copy(b.outgoing.at[lax.rem(row + k, peers)], b.arrived.at[row], b.a_send.at[k], b.a_recv.at[k], to_row(k))
 
-    def route_start(b):
+    def route_build(b, numbers):
         wide = half // 4
         i = lax.broadcasted_iota(jnp.int32, (16, spots), 1)
         j = lax.broadcasted_iota(jnp.int32, (16, spots), 0)
@@ -278,16 +284,19 @@
         hots = [
             (chosen & (eighth == (j // rollouts) * 4 + quarter)).astype(F32).astype(BF16) for quarter in range(4)
         ]
-        for n, q in enumerate(b.steps):
+        for n in numbers:
+            q = b.steps[n]
             built = jnp.zeros((spots, wide), F32)
             for quarter in range(4):
                 built = built + lax.dot_general(
                     hots[quarter],
-                    latent_rows[q, :, quarter * wide : (quarter + 1) * wide],
+                    latent_rows[q, quarter // 2, :, quarter % 2 * wide : (quarter % 2 + 1) * wide],
                     tn,
                     preferred_element_type=F32,
                 )
             b.outgoing[:, n * 16 : (n + 1) * 16, :] = built.astype(BF16).reshape(peers, 16, wide)
+
+    def route_start(b):
         for k in range(1, peers):
             route(b, k).start()
         b.arrived[row] = b.outgoing[row]
@@ -609,6 +618,12 @@
             for h in range(heads):
                 own_o[rows, h * HD : (h + 1) * HD] = summed[h * tokens : (h + 1) * tokens]
 
+        for n in (0, 1):
+
+            @pl.when(s == n + 2)
+            def _():
+                route_build(batches[0], [n])
+
         embed_actions(s + 1)
         for swap in swaps:
             swap.wait_send()
@@ -658,6 +673,7 @@
 
             @pl.when(s == STEPS - 1)
             def _():
+                route_build(batches[0], [2])
                 route_start(batches[0])
 
         reduced, sent = scatter(s, [spread_hook, route_hook])
@@ -666,7 +682,9 @@
 
         @pl.when(tensor == last)
         def _():
-            latent_rows[s] = folded(rms_rows(updated)).astype(BF16)
+            rows = folded(rms_rows(updated)).astype(BF16)
+            latent_rows[s, 0] = rows[:, : half // 2]
+            latent_rows[s, 1] = rows[:, half // 2 :]
 
         for moved in sent:
             moved.wait_send()
@@ -680,6 +698,7 @@
     spread_on(final)
     hidden_start(batches[0])
     spread_end(final)
+    route_build(batches[1], [0])
     route_start(batches[1])
     heads_start(batches[0])
     latents_ref[...] = state[...].astype(BF16)
@@ -784,14 +803,14 @@
             pltpu.VMEM((STEPS, n_z, 16, half - cut), BF16),
             pltpu.VMEM((STEPS, 16, cut), BF16),
             pltpu.VMEM((STEPS, n_z, 16, half - cut), BF16),
-            pltpu.VMEM((STEPS, 16, half), BF16),
+            pltpu.VMEM((STEPS, 2, 16, half // 2), BF16),
         ]
         + [dma((STEPS, 3, n_z))] * 2
         + [dma((STEPS, n_z + 1))] * 2
         + [dma((STEPS, 3, n_z))] * 2
         + [dma((STEPS, n_z + 1))] * 2
         + [dma((STEPS, PARTS))] * 4
-        + [dma((STEPS, n_z)), dma((STEPS, 2))]
+        + [dma((STEPS, 2, n_z)), dma((STEPS, 2, 2))]
         + [dma((6,))]
         + [ref for steps in BATCHES for ref in batch_scratch(len(steps))],
         compiler_params=pltpu.CompilerParams(

time: 258 us -> 262 us (1.016)
  Pallas kernels: 253 us -> 256 us
    pallas_call x1, Pallas kernels: 253 us -> 256 us  [shards(): pl.pallas_call(functools.partial(kernel, n_z, peers), out_shape=(jax.Shap...]
where the time goes in v6:
time: 262 us; the launch traced here: 261 us
  Pallas kernels  256 us (98%)
  local copies, waits for them, and re-layouts  4.18 us (2%)
    pallas_call x1, Pallas kernels, shards(): pl.pallas_call(functools.partial(kernel, n_z, peers), out_shape=(jax.Shap...  256 us

profile of v6, /device:TPU:8, one launch (start us, length us, event | category | flops | bytes accessed | tf_op | source)
XLA Modules:
  0.0 261.0 jit_solution(12882027603455230035)
XLA Ops:
  0.6 256.2 %imagine.1 = (bf16[8,5120]{1,0:T(8,128)(2,1)}, f32[8,4,18]{2,1,0:T(4,128)}, f32[8,4]{1,0:T(8,128)}) custom-call(bf16[8,5120]{1,0:T(8,128)(2,1)} %bitcast.9, s32[4,8]{1,0:T(4,128)} %bitcast.12, s32[1,8]{1,0:T(1,128)} %bitcast.13, f32[1,5120]{1,0:T(1,128)} %bitcast.11, bf16[18,5120]{1,0:T(8,128)(2,1)} %table_ref.1, bf16[8,1,512,256]{3,2,1,0:T(8,128)(2,1)} %cache_hbm.1, ...), custom_call_target="tpu_custom_call" | custom-call | tf_op jit(solution)/shard_map/imagine/pallas_call | solution.py:773
  256.8 1.3 copy.16
  258.1 1.5 copy.19
  259.7 1.3 copy.20

commit v7 on v6

--- a/solution.py
+++ b/solution.py
@@ -290,7 +290,7 @@
             for quarter in range(4):
                 built = built + lax.dot_general(
                     hots[quarter],
-                    latent_rows[q, quarter // 2, :, quarter % 2 * wide : (quarter % 2 + 1) * wide],
+                    latent_rows[q, 0, :, quarter * wide : (quarter + 1) * wide],
                     tn,
                     preferred_element_type=F32,
                 )
@@ -682,9 +682,7 @@
 
         @pl.when(tensor == last)
         def _():
-            rows = folded(rms_rows(updated)).astype(BF16)
-            latent_rows[s, 0] = rows[:, : half // 2]
-            latent_rows[s, 1] = rows[:, half // 2 :]
+            latent_rows[s, 0] = folded(rms_rows(updated)).astype(BF16)
 
         for moved in sent:
             moved.wait_send()
@@ -803,14 +801,14 @@
             pltpu.VMEM((STEPS, n_z, 16, half - cut), BF16),
             pltpu.VMEM((STEPS, 16, cut), BF16),
             pltpu.VMEM((STEPS, n_z, 16, half - cut), BF16),
-            pltpu.VMEM((STEPS, 2, 16, half // 2), BF16),
+            pltpu.VMEM((STEPS, 1, 16, half), BF16),
         ]
         + [dma((STEPS, 3, n_z))] * 2
         + [dma((STEPS, n_z + 1))] * 2
         + [dma((STEPS, 3, n_z))] * 2
         + [dma((STEPS, n_z + 1))] * 2
         + [dma((STEPS, PARTS))] * 4
-        + [dma((STEPS, 2, n_z)), dma((STEPS, 2, 2))]
+        + [dma((STEPS, 1, n_z)), dma((STEPS, 1, 2))]
         + [dma((6,))]
         + [ref for steps in BATCHES for ref in batch_scratch(len(steps))],
         compiler_params=pltpu.CompilerParams(

time: 262 us -> 261 us (level)
  no operation moved by 1% of the time
where the time goes in v7:
time: 261 us; the launch traced here: 260 us
  Pallas kernels  255 us (98%)
  local copies, waits for them, and re-layouts  4.18 us (2%)
    pallas_call x1, Pallas kernels, shards(): pl.pallas_call(functools.partial(kernel, n_z, peers), out_shape=(jax.Shap...  255 us

profile of v7, /device:TPU:8, one launch (start us, length us, event | category | flops | bytes accessed | tf_op | source)
XLA Modules:
  0.0 260.1 jit_solution(11442136220694265159)
XLA Ops:
  0.6 255.3 %imagine.1 = (bf16[8,5120]{1,0:T(8,128)(2,1)}, f32[8,4,18]{2,1,0:T(4,128)}, f32[8,4]{1,0:T(8,128)}) custom-call(bf16[8,5120]{1,0:T(8,128)(2,1)} %bitcast.9, s32[4,8]{1,0:T(4,128)} %bitcast.12, s32[1,8]{1,0:T(1,128)} %bitcast.13, f32[1,5120]{1,0:T(1,128)} %bitcast.11, bf16[18,5120]{1,0:T(8,128)(2,1)} %table_ref.1, bf16[8,1,512,256]{3,2,1,0:T(8,128)(2,1)} %cache_hbm.1, ...), custom_call_target="tpu_custom_call" | custom-call | tf_op jit(solution)/shard_map/imagine/pallas_call | solution.py:771
  255.9 1.3 copy.16
  257.3 1.5 copy.19
  258.8 1.3 copy.20
